TPU v7x, 256 devices: a whole 4x4x8 slice. The times are simulated.
256 devices in a mesh: tile: 64 (over z, y, core), view: 4 (over x).
Axes of the slice: x: 4, y: 4, z: 8, core: 2. Of those that a mesh axis runs over, the one named last changes fastest.
Arguments:
- measured: float32 [4, 64, 256, 256], P('view', 'tile'), may hold values from -40 to 40
- shears: int32 [4, 16, 2], P('view'), may hold values from -40 to 40, as said below
- taps: bfloat16 [4, 16, 4], P('view'), may hold values from 0 to 1, as said below
Outputs:
- volume: float32 [64, 16, 256, 256], P('tile')
- residual: float32 [4, 64, 256, 256], P('view', 'tile')
Inputs may be any that keep to these rules, and one draw needn't show every extreme that they name: In every draw some view has shears 40 and -40 along both x and y. `taps`: the two weights along x, and the two along y, each sum to one up to rounding.
All inputs are finite; a program needn't handle non-finite values.
Results may differ from a plain program's by a relative error of at most 0.007.
Values may be sent and summed in bfloat16 or wider, within the bound.
A program may use at most 64 MiB of HBM per device.

v0:
```python
import jax
import jax.numpy as jnp
from jax import lax
from jax.sharding import PartitionSpec as P

PLANES = 16
SHEAR = 40
GRID_Y = 8
ITERS = 2


tiny = 1e-06


def shifted(shard, axis, by):
    length = lax.axis_size(axis)
    pairs = [(i, i + by) for i in range(length) if 0 <= i + by < length]
    return lax.ppermute(shard, axis, pairs)


def volume_rows(blocks, amount):
    return shifted(blocks, "tile", amount)


def volume_columns(blocks, amount):
    return shifted(blocks, "tile", amount)


def image_rows(blocks, amount):
    return shifted(blocks, "tile", amount)


def image_columns(blocks, amount):
    return shifted(blocks, "tile", amount)


def extend(blocks, margin, move_rows, move_columns, grid_column):
    before = move_rows(blocks[..., -margin:, :], GRID_Y)
    after = move_rows(blocks[..., :margin, :], -GRID_Y)
    extended = jnp.concatenate([before, blocks, after], axis=-2)
    left_cols = move_columns(extended[..., -margin:], 1)
    right_cols = move_columns(extended[..., :margin], -1)
    left_cols = jnp.where(grid_column > 0, left_cols, jnp.zeros_like(left_cols))
    right_cols = jnp.where(grid_column < GRID_Y - 1, right_cols, jnp.zeros_like(right_cols))
    return jnp.concatenate([left_cols, extended, right_cols], axis=-1)


def band_stack(offset, leading, trailing, stride, rows, margin):
    extent = (rows, rows + 2 * margin)
    row_ids = lax.broadcasted_iota(jnp.int32, extent, 0)
    col_ids = lax.broadcasted_iota(jnp.int32, extent, 1)
    distance = col_ids[None, None] - row_ids[None, None] - offset[:, :, None, None]
    head_part = jnp.where(distance == 0, leading[:, :, None, None].astype(jnp.float32), 0.0)
    tail_part = jnp.where(distance == stride, trailing[:, :, None, None].astype(jnp.float32), 0.0)
    return (head_part + tail_part).astype(jnp.bfloat16)


def forward(padded, across, along, scaling):
    partial_rows = jnp.einsum(
        "zij,zjk->zik", across[0], padded, preferred_element_type=jnp.float32
    ).astype(jnp.bfloat16)
    images = [jnp.einsum("zik,zjk->ij", partial_rows, along[0], preferred_element_type=jnp.float32)]
    return jnp.stack(images)[:, None] * scaling


def backward(padded_images, across, along, scaling):
    partial_rows = jnp.einsum(
        "zij,jk->zik", across[0], padded_images[0], preferred_element_type=jnp.float32
    ).astype(jnp.bfloat16)
    view_term = jnp.einsum(
        "zik,zjk->zij", partial_rows, along[0], preferred_element_type=jnp.float32
    )
    return view_term * scaling


def local(measured, shears, taps):
    rows_x, rows_y = (measured.shape[2], measured.shape[3])
    margin = SHEAR + 1
    scaling = PLANES ** (-0.5)
    grid_column = lax.axis_index("tile") % GRID_Y
    shift_x = shears[:, :, 0]
    shift_y = shears[:, :, 1]
    across_fwd = band_stack(margin - shift_x, taps[:, :, 0], taps[:, :, 1], 1, rows_x, margin)
    along_fwd = band_stack(margin - shift_y, taps[:, :, 2], taps[:, :, 3], 1, rows_y, margin)
    across_back = band_stack(margin + shift_x, taps[:, :, 0], taps[:, :, 1], -1, rows_x, margin)
    along_back = band_stack(margin + shift_y, taps[:, :, 2], taps[:, :, 3], -1, rows_y, margin)

    def back_term(residual):
        padded_images = extend(
            residual[:, 0].astype(jnp.bfloat16), margin, image_rows, image_columns, grid_column
        )
        return backward(padded_images, across_back, along_back, scaling)

    def combine(local_term):
        return lax.psum(local_term, "view")

    def norm_of(gradient):
        return lax.psum(jnp.sum(gradient * gradient), "tile")

    residual = measured
    gradient = combine(back_term(residual))
    grad_norm = norm_of(gradient)
    direction = gradient
    volume = jnp.zeros_like(gradient)
    for rounds in range(ITERS):
        images = forward(
            extend(
                direction.astype(jnp.bfloat16), margin, volume_rows, volume_columns, grid_column
            ),
            across_fwd,
            along_fwd,
            scaling,
        )
        image_total = lax.psum(jnp.sum(images * images), ("tile", "view"))
        step_size = grad_norm / (image_total + tiny)
        volume = volume + step_size * direction
        residual = residual - step_size * images
        if rounds + 1 < ITERS:
            gradient = combine(back_term(residual))
            new_norm = norm_of(gradient)
            direction = gradient + new_norm / (grad_norm + tiny) * direction
            grad_norm = new_norm
    return (volume[None], residual)


def solution(mesh):
    placed = (P("view", "tile", None, None), P("view", None, None), P("view", None, None))
    return jax.shard_map(
        local,
        mesh=mesh,
        in_specs=placed,
        out_specs=(P("tile", None, None, None), P("view", "tile", None, None)),
        check_vma=False,
    )
```

profile of v0, /device:TPU:1, one launch (start us, length us, event | category | flops | bytes accessed | tf_op | source)
XLA Modules:
  0.0 792.2 jit_solution(17080708010023584714)
XLA Ops:
  8.2 4.4 collective-permute-start
  17.5 5.0 collective-permute-start.2
  24.5 3.9 collective-permute-done.3
  28.4 6.1 broadcast_multiply_fusion.1
  34.5 101.4 %all-reduce.3.cloned.1.call-done = f32[16,256,256]{2,1,0:T(8,128)} async-done(((f32[16,256,256]{2,1,0:T(8,128)}), f32[16,256,256]{2,1,0:T(8,128)}) %all-reduce.3.cloned.1.call-update) | async-done | bytes 4194320 | tf_op jit(solution)/shard_map/psum | solution.py:95
  135.9 5.2 multiply_reduce_fusion.1
  141.2 3.2 collective-permute-start.4
  145.7 6.4 collective-permute-done.4
  152.1 3.8 collective-permute-done.5
  158.7 2.5 copy.5
  161.3 4.9 collective-permute-start.6
  169.5 123.4 %psum.43 = f32[]{:T(128)} all-reduce(f32[]{:T(128)} %get-tuple-element.2), channel_id=1, replica_groups=mesh['tile'=64,'view'=4] {'tile'}, use_global_device_ids=true, to_apply=%region_2.3 | all-reduce | flops 1 | bytes 8 | tf_op jit(solution)/shard_map/psum | solution.py:98
  299.0 9.3 %multiply_reduce_fusion.3 = (f32[]{:T(128)}, f32[256,256]{1,0:T(8,128)S(1)}) fusion(s32[16]{0:T(128)S(1)} %get-tuple-element.21, f32[16]{0:T(128)S(1)} %get-tuple-element.26, f32[16]{0:T(128)S(1)} %get-tuple-element.27, s32[256,338]{0,1:T(8,128)} %copy-done.8, bf16[16,338,41]{2,1,0:T(8,128)(2,1)} %broadcast_select_fusion.1, ...), kind=kOutput, calls=%fused_computation.79 | convolution fusion | flops 1683966592 | bytes 4264452 | tf_op jit(solution)/shard_map/zik,zjk->ij/dot_general | solution.py:62
  308.3 80.4 %psum.44 = f32[]{:T(128)} all-reduce(f32[]{:T(128)} %get-tuple-element.28), channel_id=1, replica_groups=mesh['tile'=64,'view'=4] {'tile','view'}, use_global_device_ids=true, to_apply=%region_4.5 | all-reduce | flops 1 | bytes 8 | tf_op jit(solution)/shard_map/psum | solution.py:114
  390.1 3.7 collective-permute-start.8
  395.1 3.3 collective-permute-done.9
  398.5 4.8 collective-permute-start.10
  403.3 2.1 collective-permute-start.11
  405.5 3.6 collective-permute-done.11
  409.1 6.1 broadcast_multiply_fusion
  415.2 99.7 %all-reduce.5.cloned.1.call-done = f32[16,256,256]{2,1,0:T(8,128)} async-done(((f32[16,256,256]{2,1,0:T(8,128)}), f32[16,256,256]{2,1,0:T(8,128)}) %all-reduce.5.cloned.1.call-update) | async-done | bytes 4194320 | tf_op jit(solution)/shard_map/psum | solution.py:95
  514.9 3.9 multiply_reduce_fusion
  519.4 125.3 %psum.46 = f32[]{:T(128)} all-reduce(f32[]{:T(128)} %multiply_reduce_fusion), channel_id=1, replica_groups=mesh['tile'=64,'view'=4] {'tile'}, use_global_device_ids=true, to_apply=%region_7.8 | all-reduce | flops 1 | bytes 8 | tf_op jit(solution)/shard_map/psum | solution.py:98
  645.3 4.1 fusion.32
  652.2 3.4 collective-permute-done.12
  655.6 3.8 collective-permute-done.13
  662.2 2.5 copy.9
  664.7 4.1 collective-permute-start.14
  670.4 6.3 collective-permute-start.15
  684.0 9.2 %multiply_reduce_fusion.2 = (f32[]{:T(128)}, f32[256,256]{1,0:T(8,128)S(1)}) fusion(s32[16]{0:T(128)S(1)} %get-tuple-element.21, f32[16]{0:T(128)S(1)} %get-tuple-element.26, f32[16]{0:T(128)S(1)} %get-tuple-element.27, s32[256,338]{0,1:T(8,128)} %copy-done.8, bf16[16,338,41]{2,1,0:T(8,128)(2,1)} %broadcast_select_fusion, ...), kind=kOutput, calls=%fused_computation.78 | convolution fusion | flops 1683966592 | bytes 4264452 | tf_op jit(solution)/shard_map/zik,zjk->ij/dot_general | solution.py:62
  693.2 84.0 %psum.47 = f32[]{:T(128)} all-reduce(f32[]{:T(128)} %get-tuple-element.30), channel_id=1, replica_groups=mesh['tile'=64,'view'=4] {'tile','view'}, use_global_device_ids=true, to_apply=%region_9.10 | all-reduce | flops 1 | bytes 8 | tf_op jit(solution)/shard_map/psum | solution.py:114
  779.2 6.2 add_bitcast_fusion
  (72 shorter events, 38.3 us)
Async XLA Ops:
  7.2 128.7 %all-reduce.3.cloned.1.call-start = ((), (), s32[]{:S(2)}) async-start(), calls=%async_computation | async-start | bytes 8388608 | tf_op jit(solution)/shard_map/psum | solution.py:95
  8.2 7.3 collective-permute-start
  12.6 4.8 collective-permute-start.1
  17.5 7.0 collective-permute-start.2
  22.5 11.9 %copy-start.8 = (s32[256,338]{0,1:T(8,128)}, s32[256,338]{0,1:T(8,128)S(1)}, u32[]{:S(2)}) copy-start(s32[256,338]{0,1:T(8,128)S(1)} %iota_subtract_fusion) | copy-start | bytes 1038340
  22.6 5.8 collective-permute-start.3
  34.5 480.4 %all-reduce.5.cloned.1.call-start = ((), (), s32[]{:S(2)}) async-start(), calls=%async_computation.1 | async-start | bytes 8388608 | tf_op jit(solution)/shard_map/psum | solution.py:95
  141.2 11.0 %collective-permute-start.4 = (bf16[16,41,256]{2,1,0:T(8,128)(2,1)S(1)}, bf16[16,41,256]{2,1,0:T(8,128)(2,1)S(1)}, u32[]{:S(2)}, u32[]{:S(2)}) collective-permute-start(bf16[16,41,256]{2,1,0:T(8,128)(2,1)S(1)} %get-tuple-element.10), channel_id=1, source_target_pairs={{0,32},{4,36},{8,40},{12,44},{16,48},{20,52},{24,56},{28,60},{32,6... | collective-permute-start | bytes 1007624 | tf_op jit(solution)/shard_map/ppermute | solution.py:18
  144.4 11.6 %collective-permute-start.5 = (bf16[16,41,256]{2,1,0:T(8,128)(2,1)S(1)}, bf16[16,41,256]{2,1,0:T(8,128)(2,1)S(1)}, u32[]{:S(2)}, u32[]{:S(2)}) collective-permute-start(bf16[16,41,256]{2,1,0:T(8,128)(2,1)S(1)} %get-tuple-element.11), channel_id=1, source_target_pairs={{32,0},{36,4},{40,8},{44,12},{48,16},{52,20},{56,24},{60,28},{64,3... | collective-permute-start | bytes 1007624 | tf_op jit(solution)/shard_map/ppermute | solution.py:18
  152.1 6.6 copy-start.6
  155.9 2.8 copy-start.7
  161.3 131.7 %collective-permute-start.6 = (bf16[16,338,41]{1,0,2:T(8,128)(2,1)}, bf16[16,338,41]{1,0,2:T(8,128)(2,1)}, u32[]{:S(2)}, u32[]{:S(2)}) collective-permute-start(bf16[16,338,41]{1,0,2:T(8,128)(2,1)} %copy.5), channel_id=1, source_target_pairs={{0,4},{4,8},{8,12},{12,16},{16,20},{20,24},{24,28},{28,32},{32,36}... | collective-permute-start | bytes 1330376 | tf_op jit(solution)/shard_map/ppermute | solution.py:18
  167.6 128.4 %collective-permute-start.7 = (bf16[16,338,41]{1,0,2:T(8,128)(2,1)}, bf16[16,338,41]{1,0,2:T(8,128)(2,1)}, u32[]{:S(2)}, u32[]{:S(2)}) collective-permute-start(bf16[16,338,41]{1,0,2:T(8,128)(2,1)} %copy.7), channel_id=1, source_target_pairs={{4,0},{8,4},{12,8},{16,12},{20,16},{24,20},{28,24},{32,28},{36,32}... | collective-permute-start | bytes 1330376 | tf_op jit(solution)/shard_map/ppermute | solution.py:18
  299.0 91.0 %copy-start = (f32[1,1,256,256]{3,2,1,0:T(8,128)S(1)}, f32[1,1,256,256]{3,2,1,0:T(8,128)}, u32[]{:S(2)}) copy-start(f32[1,1,256,256]{3,2,1,0:T(8,128)} %param.3) | copy-start | bytes 786436
  299.0 110.1 %copy-start.9 = (s32[256,338]{0,1:T(8,128)S(1)}, s32[256,338]{0,1:T(8,128)}, u32[]{:S(2)}) copy-start(s32[256,338]{0,1:T(8,128)} %copy-done.8) | copy-start | bytes 1038340
  308.3 106.9 %copy-start.2 = (f32[256,256]{1,0:T(8,128)}, f32[256,256]{1,0:T(8,128)S(1)}, u32[]{:S(2)}) copy-start(f32[256,256]{1,0:T(8,128)S(1)} %get-tuple-element.29) | copy-start | bytes 786436
  390.1 5.0 collective-permute-start.8
  393.8 4.6 collective-permute-start.9
  398.5 6.9 collective-permute-start.10
  403.3 5.8 collective-permute-start.11
  649.6 6.0 collective-permute-start.12
  650.9 8.5 %collective-permute-start.13 = (bf16[16,41,256]{2,1,0:T(8,128)(2,1)S(1)}, bf16[16,41,256]{2,1,0:T(8,128)(2,1)S(1)}, u32[]{:S(2)}, u32[]{:S(2)}) collective-permute-start(bf16[16,41,256]{2,1,0:T(8,128)(2,1)S(1)} %get-tuple-element.9), channel_id=1, source_target_pairs={{32,0},{36,4},{40,8},{44,12},{48,16},{52,20},{56,24},{60,28},{64,3... | collective-permute-start | bytes 1007624 | tf_op jit(solution)/shard_map/ppermute | solution.py:18
  655.6 6.7 copy-start.4
  659.4 2.8 copy-start.5
  664.7 12.0 %collective-permute-start.14 = (bf16[16,338,41]{1,0,2:T(8,128)(2,1)}, bf16[16,338,41]{1,0,2:T(8,128)(2,1)}, u32[]{:S(2)}, u32[]{:S(2)}) collective-permute-start(bf16[16,338,41]{1,0,2:T(8,128)(2,1)} %copy.9), channel_id=1, source_target_pairs={{0,4},{4,8},{8,12},{12,16},{16,20},{20,24},{24,28},{28,32},{32,36}... | collective-permute-start | bytes 1330376 | tf_op jit(solution)/shard_map/ppermute | solution.py:18
  670.4 10.6 %collective-permute-start.15 = (bf16[16,338,41]{1,0,2:T(8,128)(2,1)}, bf16[16,338,41]{1,0,2:T(8,128)(2,1)}, u32[]{:S(2)}, u32[]{:S(2)}) collective-permute-start(bf16[16,338,41]{1,0,2:T(8,128)(2,1)} %copy.11), channel_id=1, source_target_pairs={{4,0},{8,4},{12,8},{16,12},{20,16},{24,20},{28,24},{32,28},{36,32}... | collective-permute-start | bytes 1330376 | tf_op jit(solution)/shard_map/ppermute | solution.py:18
  684.0 94.5 %copy-start.1 = (f32[1,1,256,256]{3,2,1,0:T(8,128)S(1)}, f32[1,1,256,256]{3,2,1,0:T(8,128)}, u32[]{:S(2)}) copy-start(f32[1,1,256,256]{3,2,1,0:T(8,128)} %param.3) | copy-start | bytes 786436
  684.0 94.5 %copy-start.3 = (f32[256,256]{1,0:T(8,128)S(1)}, f32[256,256]{1,0:T(8,128)}, u32[]{:S(2)}) copy-start(f32[256,256]{1,0:T(8,128)} %copy-done.2) | copy-start | bytes 786436
Sparse Core Ops, SparseCore 0:
  34.6 101.2 all-reduce.2
  415.3 99.4 all-reduce.4
where the time goes:
time: 793 us; the launch traced here: 792 us
  blocking collectives  413 us (52%)
  waiting for transfers between devices  232 us (29%)
  starting transfers between devices  48.8 us (6%)
  matrix products  30.6 us (4%)
  other arithmetic  29.9 us (4%)
  local copies, waits for them, and re-layouts  19.3 us (2%)
  between operations  18.2 us (2%)
    psum x2, blocking collectives, norm_of(): return lax.psum(jnp.sum(gradient * gradient), 'tile')  249 us
    psum x2, waiting for transfers between devices, combine(): return lax.psum(local_term, 'view')  201 us
    psum x2, blocking collectives, local(): image_total = lax.psum(jnp.sum(images * images), ('tile', 'view'))  164 us
    ppermute x16, starting transfers between devices, shifted(): return lax.ppermute(shard, axis, pairs)  48.8 us
    ppermute x16, waiting for transfers between devices, shifted(): return lax.ppermute(shard, axis, pairs)  31.3 us
    dot_general x2, matrix products, forward(): jnp.einsum('zik,zjk->ij', partial_rows, along[0], preferred_element_type=...  18.5 us
  transfers between devices with their start and end apart: 18, of which 11 were waited for; matrix products, arithmetic and copies ran while one was open for 1% of the time, Pallas kernels for 0%

commit v1 on v0

v1 whole, which is shorter than its diff:
```python
import functools

import jax
import jax.numpy as jnp
from jax import lax
from jax.experimental import pallas as pl
from jax.experimental.pallas import tpu as pltpu
from jax.sharding import PartitionSpec as P

PLANES = 16
VIEWS = 4
GRID_Y = 8
TX = 256
TY = 256
HX = 96
HY = 128
RX = TX + 2 * HX
RY = TY + 2 * HY
VX = 48
VROWS = RX - 2 * VX
WINDOW = 288
T_ROWS = 384
BACK_WINDOW = 272
FAR = 1 << 20
TINY = 1e-6
MESH = pl.DeviceIdType.MESH

X_SEMS = 6
Z_BASE = X_SEMS
Y_BASE = Z_BASE + 2 * VIEWS
N_SEMS = Y_BASE + 8 * VIEWS

PARTS = {"a": (HX, TX // 2), "b": (HX + TX // 2, TX // 2), "top": (0, HX), "bottom": (HX + TX, HX)}
PART_ID = {"a": 0, "b": 1, "top": 2, "bottom": 3}


def ring(index, step, size):
    return lax.rem(index + (step + size), size)


def solve_kernel(
    grid_x,
    meas_ref, sh_ref, tp_ref,
    yext_ref, res_ref, sh_s, tp_s,
    e_refs, f_refs, r_refs, y_ref, x_ref, t_refs, q_ref, h_ref,
    sh_v, tp_v, ra_ref, rb_ref, rc_ref,
    send_sems, recv_sems, p_send, p_recv, p_local, a_send, a_recv,
):
    tile = lax.axis_index("tile")
    view = lax.axis_index("view")
    gx = tile // GRID_Y
    gy = lax.rem(tile, GRID_Y)

    def at(row, col, vw):
        return (row * GRID_Y + col, vw)

    def to_view(step):
        return at(gx, gy, ring(view, step, VIEWS))

    def to_row(step):
        return at(ring(gx, step, grid_x), gy, view)

    def to_col(step):
        return at(gx, ring(gy, step, GRID_Y), view)

    partners = (
        [to_view(s) for s in range(1, VIEWS)]
        + [to_row(s) for s in range(1, grid_x)]
        + [to_col(s) for s in range(1, GRID_Y)]
    )
    barrier = pltpu.get_barrier_semaphore()
    for partner in partners:
        pl.semaphore_signal(barrier, inc=1, device_id=partner, device_id_type=MESH)

    e_refs[0][pl.ds(HX, TX), pl.ds(HY, TY)] = meas_ref[0, 0].astype(jnp.bfloat16)
    sh_v[0] = jnp.zeros((PLANES, 128), jnp.int32)
    sh_v[0, :, 0:2] = sh_ref[0]
    tp_v[0] = jnp.zeros((PLANES, 128), jnp.float32)
    tp_v[0, :, 0:4] = tp_ref[0].astype(jnp.float32)

    pl.semaphore_wait(barrier, len(partners))

    parameter_copies = []
    for step in range(1, VIEWS):
        slot = VIEWS - step
        for which, ref in ((0, sh_v), (1, tp_v)):
            copy = pltpu.make_async_remote_copy(
                src_ref=ref.at[0], dst_ref=ref.at[slot],
                send_sem=p_send.at[which, slot], recv_sem=p_recv.at[which, slot],
                device_id=to_view(step), device_id_type=MESH,
            )
            copy.start()
            parameter_copies.append(copy)

    class Exchange:
        def __init__(self, bufs, which):
            self.bufs, self.which, self.copies = bufs, which, {}

        def send(self, key, sem, src, dst, device):
            copy = pltpu.make_async_remote_copy(
                src_ref=src, dst_ref=dst,
                send_sem=send_sems.at[self.which, sem], recv_sem=recv_sems.at[self.which, sem],
                device_id=device, device_id_type=MESH,
            )
            copy.start()
            self.copies[key] = copy

        def region(self, slot, rows, cols):
            return self.bufs[slot].at[pl.ds(*rows), pl.ds(*cols)]

        def along_view(self, src_slot, dst_slot, part, sem, step):
            rows = PARTS[part]
            self.send(
                ("x", dst_slot, part), sem,
                self.region(src_slot, rows, (HY, TY)), self.region(dst_slot, rows, (HY, TY)),
                to_view(step),
            )

        def begin(self):
            self.along_view(0, 3, "a", 0, 1)
            self.along_view(0, 1, "b", 1, -1)
            self.along_view(0, 3, "b", 2, 1)
            self.along_view(0, 1, "a", 3, -1)
            self.spread(0, "a")
            self.spread(0, "b")

        def columns(self, slot, part):
            rows = PARTS[part]
            sem = Y_BASE + 8 * slot + 2 * PART_ID[part]
            self.send(
                ("y", slot, part, 0), sem,
                self.region(slot, rows, (HY, HY)), self.region(slot, rows, (HY + TY, HY)), to_col(-1),
            )
            self.send(
                ("y", slot, part, 1), sem + 1,
                self.region(slot, rows, (TY, HY)), self.region(slot, rows, (0, HY)), to_col(1),
            )

        def spread(self, slot, part):
            if part == "a":
                self.send(
                    ("z", slot, "bottom"), Z_BASE + 2 * slot,
                    self.region(slot, (HX, HX), (HY, TY)),
                    self.region(slot, (HX + TX, HX), (HY, TY)), to_row(-1),
                )
            else:
                self.send(
                    ("z", slot, "top"), Z_BASE + 2 * slot + 1,
                    self.region(slot, (TX, HX), (HY, TY)),
                    self.region(slot, (0, HX), (HY, TY)), to_row(1),
                )
            self.columns(slot, part)

        def arrive(self, slot, part):
            self.copies["x", slot, part].wait_recv()
            if slot == 3 and part == "a":
                self.along_view(3, 2, "a", 4, 1)
            if slot == 1 and part == "b":
                self.along_view(1, 2, "b", 5, -1)
            self.spread(slot, part)

        def corners(self, slot):
            for part, edge in (("top", 0), ("bottom", grid_x - 1)):
                self.copies["z", slot, part].wait_recv()

                @pl.when(gx == edge)
                def _():
                    start, size = PARTS[part]
                    self.bufs[slot][pl.ds(start, size), pl.ds(HY, TY)] = jnp.zeros((size, TY), jnp.bfloat16)

                self.columns(slot, part)

        def complete(self, slot):
            for part in PARTS:
                for side in (0, 1):
                    self.copies["y", slot, part, side].wait_recv()
            for side, edge in ((0, 0), (HY + TY, GRID_Y - 1)):
                @pl.when(gy == edge)
                def _():
                    self.bufs[slot][:, pl.ds(side, HY)] = jnp.zeros((RX, HY), jnp.bfloat16)

        def finish(self):
            for copy in self.copies.values():
                copy.wait_send()

    first = Exchange(e_refs, 0)
    first.begin()

    def clear(pair, carry):
        y_ref[pair, 0:32, 0:128] = jnp.zeros((32, 128), jnp.bfloat16)
        y_ref[pair, 352:512, 0:128] = jnp.zeros((160, 128), jnp.bfloat16)
        y_ref[pair, 0:160, 128:256] = jnp.zeros((160, 128), jnp.bfloat16)
        y_ref[pair, 480:512, 128:256] = jnp.zeros((32, 128), jnp.bfloat16)
        x_ref[pair, 0:96, 128:256] = jnp.zeros((96, 128), jnp.bfloat16)
        x_ref[pair, 128:224, 128:256] = jnp.zeros((96, 128), jnp.bfloat16)
        return carry

    lax.fori_loop(0, VIEWS * PLANES, clear, 0)
    for t_ref in t_refs:
        t_ref[WINDOW:, :] = jnp.zeros((T_ROWS - WINDOW, TY), jnp.bfloat16)

    for copy in parameter_copies:
        copy.wait_recv()
    local = [pltpu.make_async_copy(sh_v, sh_s, p_local.at[0]), pltpu.make_async_copy(tp_v, tp_s, p_local.at[1])]
    for copy in local:
        copy.start()
    for copy in local:
        copy.wait()

    column_low = jnp.where(gy == 0, 0, -FAR)
    column_high = jnp.where(gy == GRID_Y - 1, TY, FAR)
    row_low = jnp.where(gx == 0, 0, -FAR)
    row_high = jnp.where(gx == grid_x - 1, TX, FAR)

    def build(slot):
        def one(z, carry):
            shear = sh_s[0, z, 1]
            d = sh_s[slot, z, 1] - shear
            a0, a1 = tp_s[0, z, 2], tp_s[0, z, 3]
            b0, b1 = tp_s[slot, z, 2], tp_s[slot, z, 3]
            col = lax.broadcasted_iota(jnp.int32, (1, 128), 1)
            distance = (
                lax.broadcasted_iota(jnp.int32, (320, 128), 0)
                - lax.broadcasted_iota(jnp.int32, (320, 128), 1)
                + (32 - HY)
            )
            hit = [distance == d + k for k in (-1, 0, 1)]
            low, high = shear + column_low, shear + column_high
            for tile_start, in0, in1 in (
                (0, col >= low, col >= low - 1),
                (128, col + 128 < high, col + 128 < high - 1),
            ):
                before = jnp.where(in0, a0 * b1, 0.0)
                middle = jnp.where(in0, a0 * b0, 0.0) + jnp.where(in1, a1 * b1, 0.0)
                after = jnp.where(in1, a1 * b0, 0.0)
                value = jnp.where(hit[0], before, jnp.where(hit[1], middle, jnp.where(hit[2], after, 0.0)))
                y_ref[slot * PLANES + z, pl.ds(32 + tile_start, 320), pl.ds(tile_start, 128)] = value.astype(
                    jnp.bfloat16
                )

            shear = sh_s[0, z, 0]
            first_row = HX - 1 + sh_s[slot, z, 0] - shear
            m = first_row - lax.shift_left(lax.shift_right_logical(first_row, 4), 4)
            a0, a1 = tp_s[0, z, 0] * (1.0 / PLANES), tp_s[0, z, 1] * (1.0 / PLANES)
            b0, b1 = tp_s[slot, z, 0], tp_s[slot, z, 1]
            low, high = shear + row_low, shear + row_high
            for row_start, size, col_start in ((0, 128, 0), (96, 32, 128)):
                row = lax.broadcasted_iota(jnp.int32, (size, 128), 0) + row_start
                distance = lax.broadcasted_iota(jnp.int32, (size, 128), 1) - row + col_start
                hit = [distance == m + k for k in (0, 1, 2)]
                for half, in0, in1 in (
                    (0, row >= low, row >= low - 1),
                    (128, row + 128 < high, row + 128 < high - 1),
                ):
                    before = jnp.where(in0, a0 * b1, 0.0)
                    middle = jnp.where(in0, a0 * b0, 0.0) + jnp.where(in1, a1 * b1, 0.0)
                    after = jnp.where(in1, a1 * b0, 0.0)
                    value = jnp.where(hit[0], before, jnp.where(hit[1], middle, jnp.where(hit[2], after, 0.0)))
                    x_ref[slot * PLANES + z, pl.ds(half + row_start, size), pl.ds(col_start, 128)] = value.astype(
                        jnp.bfloat16
                    )
            return carry

        lax.fori_loop(0, PLANES, one, 0)

    def apply(src_ref, out_ref, slot):
        def group(g, carry):
            top, bottom = out_ref[0:128, :], out_ref[128:256, :]
            for u, t_ref in enumerate(t_refs):
                z = len(t_refs) * g + u
                pair = slot * PLANES + z
                first_row = HX - 1 + sh_s[slot, z, 0] - sh_s[0, z, 0]
                start = lax.shift_right_logical(first_row, 4) * 16
                t_ref[0:WINDOW, :] = jnp.dot(
                    src_ref[pl.ds(start, WINDOW), :], y_ref[pair], preferred_element_type=jnp.float32
                ).astype(jnp.bfloat16)
                top = top + jnp.dot(x_ref[pair, 0:128, :], t_ref[0:256, :], preferred_element_type=jnp.float32)
                bottom = bottom + jnp.dot(
                    x_ref[pair, 128:256, :], t_ref[128:384, :], preferred_element_type=jnp.float32
                )
            out_ref[0:128, :], out_ref[128:256, :] = top, bottom
            return carry

        lax.fori_loop(0, PLANES // len(t_refs), group, 0)

    def lanes(x):
        s = jnp.sum(x, axis=0, keepdims=True)
        return s[:, 0:128] + s[:, 128:256]

    class Sum:
        def __init__(self, which, rows):
            self.which = which
            self.stages = (
                (ra_ref, view, VIEWS, to_view, 0),
                (rb_ref, gy, GRID_Y, to_col, VIEWS),
                (rc_ref, gx, grid_x, to_row, VIEWS + GRID_Y),
            )
            self.copies = []
            pad = jnp.zeros((8 - len(rows), 128), jnp.float32)
            self.value = jnp.concatenate(list(rows) + [pad], axis=0)

        def send(self, stage):
            ref, me, size, to, base = self.stages[stage]
            ref[self.which, me] = self.value
            self.current = []
            for step in range(1, size):
                copy = pltpu.make_async_remote_copy(
                    src_ref=ref.at[self.which, me], dst_ref=ref.at[self.which, me],
                    send_sem=a_send.at[self.which, base + step], recv_sem=a_recv.at[self.which, base + step],
                    device_id=to(step), device_id_type=MESH,
                )
                copy.start()
                self.current.append(copy)
            self.copies += self.current

        def receive(self, stage):
            ref, me, size, to, base = self.stages[stage]
            for copy in self.current:
                copy.wait_recv()
            total = ref[self.which, 0]
            for i in range(1, size):
                total = total + ref[self.which, i]
            self.value = total

        def row(self, i):
            return jnp.sum(self.value[i : i + 1, :], axis=1, keepdims=True)

        def finish(self):
            for copy in self.copies:
                copy.wait_send()

    q_ref[...] = jnp.zeros((TX, TY), jnp.float32)
    h_ref[...] = jnp.zeros((TX, TY), jnp.float32)

    build(0)
    first.arrive(3, "a")
    first.arrive(1, "b")
    first.arrive(3, "b")
    first.arrive(1, "a")
    first.corners(0)
    build(3)
    first.corners(3)
    first.corners(1)
    first.arrive(2, "a")
    first.arrive(2, "b")
    build(1)
    first.corners(2)
    build(2)
    for slot in (0, 3, 1, 2):
        first.complete(slot)
        apply(e_refs[slot], q_ref, slot)

    second = Exchange(f_refs, 1)
    f_refs[0][pl.ds(HX, TX), pl.ds(HY, TY)] = q_ref[...].astype(jnp.bfloat16)
    second.begin()
    q0 = q_ref[...]
    r0 = e_refs[0][pl.ds(HX, TX), pl.ds(HY, TY)].astype(jnp.float32)
    sums = Sum(0, [lanes(r0 * q0), lanes(q0 * q0)])
    sums.send(0)
    sums.receive(0)
    sums.send(1)
    second.arrive(3, "a")
    second.arrive(1, "b")
    second.arrive(3, "b")
    second.arrive(1, "a")
    second.corners(0)
    sums.receive(1)
    sums.send(2)
    second.corners(3)
    second.corners(1)
    second.arrive(2, "a")
    second.arrive(2, "b")
    sums.receive(2)
    gamma0, norm0 = sums.row(0), sums.row(1)
    alpha0 = gamma0 / (norm0 + TINY)
    second.corners(2)

    def update(slot):
        for start in range(0, RX, 64):
            rows = pl.ds(start, 64)
            r_refs[slot][rows, :] = (
                e_refs[slot][rows, :].astype(jnp.float32) - alpha0 * f_refs[slot][rows, :].astype(jnp.float32)
            ).astype(jnp.bfloat16)

    for slot in (0, 3, 1, 2):
        second.complete(slot)
        update(slot)
        apply(r_refs[slot], h_ref, slot)

    h1 = h_ref[...]
    q0 = q_ref[...]
    r1 = r_refs[0][pl.ds(HX, TX), pl.ds(HY, TY)].astype(jnp.float32)
    sums2 = Sum(1, [lanes(r1 * h1), lanes(h1 * h1), lanes(h1 * q0)])
    for stage in range(3):
        sums2.send(stage)
        sums2.receive(stage)
    gamma1 = sums2.row(0)
    beta = gamma1 / (gamma0 + TINY)
    norm1 = sums2.row(1) + 2.0 * beta * sums2.row(2) + beta * beta * norm0
    alpha1 = gamma1 / (norm1 + TINY)
    weight0 = alpha0 + alpha1 * beta

    q0 = q_ref[...]
    res_ref[0, 0] = meas_ref[0, 0] - alpha0 * q0 - alpha1 * (h_ref[...] + beta * q0)
    for slot in range(VIEWS):
        for start in range(0, VROWS, 32):
            rows = pl.ds(VX + start, 32)
            yext_ref[slot, pl.ds(start, 32), :] = (
                weight0 * e_refs[slot][rows, :].astype(jnp.float32)
                + alpha1 * r_refs[slot][rows, :].astype(jnp.float32)
            ).astype(jnp.bfloat16)

    for copy in parameter_copies:
        copy.wait_send()
    first.finish()
    second.finish()
    sums.finish()
    sums2.finish()


def volume_kernel(sh_s, tp_s, y_ref, res_in, vol_ref, res_out, b_ref, x_ref, t_ref):
    view = lax.axis_index("view")
    z = pl.program_id(0)

    @pl.when(z == 0)
    def _():
        b_ref[...] = jnp.zeros(b_ref.shape, jnp.bfloat16)
        x_ref[...] = jnp.zeros(x_ref.shape, jnp.bfloat16)
        t_ref[...] = jnp.zeros(t_ref.shape, jnp.bfloat16)
        res_out[...] = res_in[...]

    top = bottom = None
    for v in range(VIEWS):
        slot = lax.rem(v - view + VIEWS, VIEWS)
        d = sh_s[slot, z, 1]
        distance = (
            lax.broadcasted_iota(jnp.int32, (224, 128), 0)
            - lax.broadcasted_iota(jnp.int32, (224, 128), 1)
            + (80 - HY)
        )
        value = jnp.where(
            distance == d, tp_s[slot, z, 2], jnp.where(distance == d - 1, tp_s[slot, z, 3], 0.0)
        ).astype(jnp.bfloat16)
        b_ref[v, 80:304, 0:128] = value
        b_ref[v, 208:432, 128:256] = value
        first_row = HX - VX - 1 + sh_s[slot, z, 0]
        start = pl.multiple_of(lax.shift_left(lax.shift_right_logical(first_row, 4), 4), 16)
        m = first_row - start
        b0, b1 = tp_s[slot, z, 0] * (PLANES**-0.5), tp_s[slot, z, 1] * (PLANES**-0.5)
        for row_start, size, col_start in ((0, 128, 0), (96, 32, 128)):
            distance = (
                lax.broadcasted_iota(jnp.int32, (size, 128), 1)
                - lax.broadcasted_iota(jnp.int32, (size, 128), 0)
                + (col_start - row_start)
            )
            x_ref[v, pl.ds(row_start, size), pl.ds(col_start, 128)] = jnp.where(
                distance == m, b1, jnp.where(distance == m + 1, b0, 0.0)
            ).astype(jnp.bfloat16)
        t_ref[v, 0:BACK_WINDOW, :] = jnp.dot(
            y_ref[slot, pl.ds(start, BACK_WINDOW), :], b_ref[v], preferred_element_type=jnp.float32
        ).astype(jnp.bfloat16)
        upper = jnp.dot(x_ref[v], t_ref[v, 0:256, :], preferred_element_type=jnp.float32)
        lower = jnp.dot(x_ref[v], t_ref[v, 128:384, :], preferred_element_type=jnp.float32)
        top = upper if top is None else top + upper
        bottom = lower if bottom is None else bottom + lower
    vol_ref[0, 0, 0:128, :] = top
    vol_ref[0, 0, 128:256, :] = bottom


def local(grid_x, measured, shears, taps):
    f32, bf16 = jnp.float32, jnp.bfloat16
    vmem = pl.BlockSpec(memory_space=pltpu.VMEM)
    smem = pl.BlockSpec(memory_space=pltpu.SMEM)
    yext, partial, sh_all, tp_all = pl.pallas_call(
        functools.partial(solve_kernel, grid_x),
        name="solve",
        out_shape=(
            jax.ShapeDtypeStruct((VIEWS, VROWS, RY), bf16),
            jax.ShapeDtypeStruct((1, 1, TX, TY), f32),
            jax.ShapeDtypeStruct((VIEWS, PLANES, 128), jnp.int32),
            jax.ShapeDtypeStruct((VIEWS, PLANES, 128), f32),
        ),
        in_specs=[vmem, vmem, vmem],
        out_specs=(vmem, vmem, smem, smem),
        scratch_shapes=[
            [pltpu.VMEM((RX, RY), bf16)] * VIEWS,
            [pltpu.VMEM((RX, RY), bf16)] * VIEWS,
            [pltpu.VMEM((RX, RY), bf16)] * VIEWS,
            pltpu.VMEM((VIEWS * PLANES, RY, TY), bf16),
            pltpu.VMEM((VIEWS * PLANES, TX, 256), bf16),
            [pltpu.VMEM((T_ROWS, TY), bf16)] * 4,
            pltpu.VMEM((TX, TY), f32),
            pltpu.VMEM((TX, TY), f32),
            pltpu.VMEM((VIEWS, PLANES, 128), jnp.int32),
            pltpu.VMEM((VIEWS, PLANES, 128), f32),
            pltpu.VMEM((2, VIEWS, 8, 128), f32),
            pltpu.VMEM((2, GRID_Y, 8, 128), f32),
            pltpu.VMEM((2, grid_x, 8, 128), f32),
            pltpu.SemaphoreType.DMA((2, N_SEMS)),
            pltpu.SemaphoreType.DMA((2, N_SEMS)),
            pltpu.SemaphoreType.DMA((2, VIEWS)),
            pltpu.SemaphoreType.DMA((2, VIEWS)),
            pltpu.SemaphoreType.DMA((2,)),
            pltpu.SemaphoreType.DMA((2, VIEWS + GRID_Y + grid_x)),
            pltpu.SemaphoreType.DMA((2, VIEWS + GRID_Y + grid_x)),
        ],
        compiler_params=pltpu.CompilerParams(
            collective_id=0, has_side_effects=True, vmem_limit_bytes=48 * 1024 * 1024
        ),
    )(measured, shears, taps)
    volume, residual = pl.pallas_call(
        volume_kernel,
        name="back_project",
        grid=(PLANES,),
        out_shape=(
            jax.ShapeDtypeStruct((1, PLANES, TX, TY), f32),
            jax.ShapeDtypeStruct((1, 1, TX, TY), f32),
        ),
        in_specs=[smem, smem, vmem, vmem],
        out_specs=(
            pl.BlockSpec((1, 1, TX, TY), lambda z: (0, z, 0, 0)),
            pl.BlockSpec((1, 1, TX, TY), lambda z: (0, 0, 0, 0)),
        ),
        scratch_shapes=[
            pltpu.VMEM((VIEWS, RY, TY), bf16),
            pltpu.VMEM((VIEWS, 128, 256), bf16),
            pltpu.VMEM((VIEWS, T_ROWS, TY), bf16),
        ],
        compiler_params=pltpu.CompilerParams(vmem_limit_bytes=32 * 1024 * 1024),
    )(sh_all, tp_all, yext, partial)
    return volume, residual


def solution(mesh):
    placed = (P("view", "tile", None, None), P("view", None, None), P("view", None, None))
    return jax.shard_map(
        functools.partial(local, mesh.shape["tile"] // GRID_Y),
        mesh=mesh,
        in_specs=placed,
        out_specs=(P("tile", None, None, None), P("view", "tile", None, None)),
        check_vma=False,
    )
```

time: 793 us -> 115 us (0.15)
  blocking collectives: 413 us -> 0 us
  waiting for transfers between devices: 232 us -> 0 us
  Pallas kernels: 0 us -> 112 us
  starting transfers between devices: 48.8 us -> 0 us
  matrix products: 30.6 us -> 0 us
  other arithmetic: 29.9 us -> 0 us
  between operations: 18.2 us -> 0.64 us
  local copies, waits for them, and re-layouts: 19.3 us -> 2.47 us
    psum x4 -> x0, blocking collectives: 413 us -> none  [the longest x2 249 us: norm_of(): return lax.psum(jnp.sum(gradient * gradient), 'tile')]
    psum x2 -> x0, waiting for transfers between devices: 201 us -> none  [combine(): return lax.psum(local_term, 'view')]
    pallas_call x0 -> x2, Pallas kernels: none -> 112 us  [the longest x1 90.2 us: local(): pl.pallas_call(functools.partial(solve_kernel, grid_x), name='solve', out...]
    ppermute x16 -> x0, starting transfers between devices: 48.8 us -> none  [shifted(): return lax.ppermute(shard, axis, pairs)]
    ppermute x16 -> x0, waiting for transfers between devices: 31.3 us -> none  [shifted(): return lax.ppermute(shard, axis, pairs)]
    dot_general x4 -> x0, matrix products: 30.6 us -> none  [the longest x2 18.5 us: forward(): jnp.einsum('zik,zjk->ij', partial_rows, along[0], preferred_element_type=...]
    slice x12 -> x0, local copies, waits for them, and re-layouts: 11.9 us -> none  [the longest x6 8.66 us: extend(): left_cols = move_columns(extended[..., -margin:], 1)]
    reduce_sum x2 -> x0, other arithmetic: 9.02 us -> none  [norm_of(): return lax.psum(jnp.sum(gradient * gradient), 'tile')]
  transfers between devices with their start and end apart: 18 -> 0, of which waited for: 11 -> 0; matrix products, arithmetic and copies ran while one was open for 1% -> 0% of each run, Pallas kernels for 0% -> 0%
where the time goes in v1:
time: 115 us
  Pallas kernels  112 us (97%)
  local copies, waits for them, and re-layouts  2.47 us (2%)
    pallas_call x1, Pallas kernels, local(): pl.pallas_call(functools.partial(solve_kernel, grid_x), name='solve', out...  90.2 us
    pallas_call x1, Pallas kernels, local(): pl.pallas_call(volume_kernel, name='back_project', grid=(PLANES,), out_sh...  21.4 us
    unnamed x4, local copies, waits for them, and re-layouts  2.47 us

profile of v1, /device:TPU:1, one launch (start us, length us, event | category | flops | bytes accessed | tf_op | source)
XLA Modules:
  0.0 114.7 jit_solution(13581359521030595371)
XLA Ops:
  0.6 0.8 copy.6.tp_ref
  1.4 0.8 copy.5.sh_ref
  2.2 0.0 copy-start
  2.2 0.9 copy-done
  3.1 90.2 %solve.1 = (bf16[4,352,512]{2,1,0:T(8,128)(2,1)S(1)}, f32[1,1,256,256]{3,2,1,0:T(8,128)S(1)}, s32[4,16,128]{2,1,0:T(8,128)S(1)}, f32[4,16,128]{2,1,0:T(8,128)S(1)}) custom-call(f32[1,1,256,256]{3,2,1,0:T(8,128)S(1)} %copy-done, s32[1,16,2]{2,1,0:T(8,128)S(1)} %copy.5.sh_ref, bf16[1,16,4]{2,1,0:T(8,128)(2,1)S(1)} %copy.6.tp_ref), custom_call_target="tpu_custom_call" | custom-call | tf_op jit(solution)/shard_map/solve/pallas_call | solution.py:474
  93.3 21.4 %back_project.1 = (f32[1,16,256,256]{3,2,1,0:T(8,128)}, f32[1,1,256,256]{3,2,1,0:T(8,128)}) custom-call(s32[4,16,128]{2,1,0:T(8,128)S(1)} %get-tuple-element.6.sh_s, f32[4,16,128]{2,1,0:T(8,128)S(1)} %get-tuple-element.7.tp_s, bf16[4,352,512]{2,1,0:T(8,128)(2,1)S(1)} %get-tuple-element.8.y_ref, f32[1,1,256,256]{3,2,1,0:T(8,128)S(1)} %get-tuple-element.9.res_in), custom_call_target="tpu_custom_call" | custom-call | tf_op jit(solution)/shard_map/back_project/pallas_call | solution.py:511
Async XLA Ops:
  2.2 0.9 copy-start

commit v2 on v1

--- a/solution.py
+++ b/solution.py
@@ -17,10 +17,16 @@
 RX = TX + 2 * HX
 RY = TY + 2 * HY
 VX = 48
-VROWS = RX - 2 * VX
+VROWS = RX - VX - 32
 WINDOW = 288
-T_ROWS = 384
-BACK_WINDOW = 272
+BACK_WINDOW = 288
+STRIP = 160
+BACK_PLANES = 4
+GROUP = 4
+BAND = (
+    (0, 0, 0, 128), (0, 1, 96, 32), (1, 1, 0, 96), (1, 2, 64, 64),
+    (2, 2, 0, 64), (2, 3, 32, 96), (3, 3, 0, 32), (3, 4, 0, 128),
+)
 FAR = 1 << 20
 TINY = 1e-6
 MESH = pl.DeviceIdType.MESH
@@ -42,7 +48,7 @@
     grid_x,
     meas_ref, sh_ref, tp_ref,
     yext_ref, res_ref, sh_s, tp_s,
-    e_refs, f_refs, r_refs, y_ref, x_ref, t_refs, q_ref, h_ref,
+    e_refs, f_refs, r_refs, y_ref, x_ref, upper_ref, lower_ref, q_ref, h_ref,
     sh_v, tp_v, ra_ref, rb_ref, rc_ref,
     send_sems, recv_sems, p_send, p_recv, p_local, a_send, a_recv,
 ):
@@ -191,13 +197,9 @@
         y_ref[pair, 352:512, 0:128] = jnp.zeros((160, 128), jnp.bfloat16)
         y_ref[pair, 0:160, 128:256] = jnp.zeros((160, 128), jnp.bfloat16)
         y_ref[pair, 480:512, 128:256] = jnp.zeros((32, 128), jnp.bfloat16)
-        x_ref[pair, 0:96, 128:256] = jnp.zeros((96, 128), jnp.bfloat16)
-        x_ref[pair, 128:224, 128:256] = jnp.zeros((96, 128), jnp.bfloat16)
         return carry
 
     lax.fori_loop(0, VIEWS * PLANES, clear, 0)
-    for t_ref in t_refs:
-        t_ref[WINDOW:, :] = jnp.zeros((T_ROWS - WINDOW, TY), jnp.bfloat16)
 
     for copy in parameter_copies:
         copy.wait_recv()
@@ -237,51 +239,57 @@
                 y_ref[slot * PLANES + z, pl.ds(32 + tile_start, 320), pl.ds(tile_start, 128)] = value.astype(
                     jnp.bfloat16
                 )
-
-            shear = sh_s[0, z, 0]
-            first_row = HX - 1 + sh_s[slot, z, 0] - shear
-            m = first_row - lax.shift_left(lax.shift_right_logical(first_row, 4), 4)
-            a0, a1 = tp_s[0, z, 0] * (1.0 / PLANES), tp_s[0, z, 1] * (1.0 / PLANES)
-            b0, b1 = tp_s[slot, z, 0], tp_s[slot, z, 1]
-            low, high = shear + row_low, shear + row_high
-            for row_start, size, col_start in ((0, 128, 0), (96, 32, 128)):
+            return carry
+
+        lax.fori_loop(0, PLANES, one, 0)
+
+    def build_rows(slot):
+        def one(g, carry):
+            scalars = []
+            for u in range(GROUP):
+                z = GROUP * g + u
+                shear = sh_s[0, z, 0]
+                first_row = HX - 1 + sh_s[slot, z, 0] - shear
+                m = first_row - lax.shift_right_logical(first_row, 4) * 16 + STRIP * u
+                a0, a1 = tp_s[0, z, 0] * (1.0 / PLANES), tp_s[0, z, 1] * (1.0 / PLANES)
+                b0, b1 = tp_s[slot, z, 0], tp_s[slot, z, 1]
+                scalars.append((m, a0 * b1, a0 * b0, a1 * b1, a1 * b0, shear + row_low, shear + row_high))
+            for u, block, row_start, size in BAND:
+                m, am, az, bz, bp, low, high = scalars[u]
                 row = lax.broadcasted_iota(jnp.int32, (size, 128), 0) + row_start
-                distance = lax.broadcasted_iota(jnp.int32, (size, 128), 1) - row + col_start
+                distance = lax.broadcasted_iota(jnp.int32, (size, 128), 1) - row + 128 * block
                 hit = [distance == m + k for k in (0, 1, 2)]
                 for half, in0, in1 in (
                     (0, row >= low, row >= low - 1),
-                    (128, row + 128 < high, row + 128 < high - 1),
+                    (1, row + 128 < high, row + 128 < high - 1),
                 ):
-                    before = jnp.where(in0, a0 * b1, 0.0)
-                    middle = jnp.where(in0, a0 * b0, 0.0) + jnp.where(in1, a1 * b1, 0.0)
-                    after = jnp.where(in1, a1 * b0, 0.0)
+                    before = jnp.where(in0, am, 0.0)
+                    middle = jnp.where(in0, az, 0.0) + jnp.where(in1, bz, 0.0)
+                    after = jnp.where(in1, bp, 0.0)
                     value = jnp.where(hit[0], before, jnp.where(hit[1], middle, jnp.where(hit[2], after, 0.0)))
-                    x_ref[slot * PLANES + z, pl.ds(half + row_start, size), pl.ds(col_start, 128)] = value.astype(
-                        jnp.bfloat16
-                    )
+                    x_ref[slot, half, g, pl.ds(row_start, size), pl.ds(128 * block, 128)] = value.astype(jnp.bfloat16)
             return carry
 
-        lax.fori_loop(0, PLANES, one, 0)
+        lax.fori_loop(0, PLANES // GROUP, one, 0)
 
     def apply(src_ref, out_ref, slot):
-        def group(g, carry):
-            top, bottom = out_ref[0:128, :], out_ref[128:256, :]
-            for u, t_ref in enumerate(t_refs):
-                z = len(t_refs) * g + u
-                pair = slot * PLANES + z
-                first_row = HX - 1 + sh_s[slot, z, 0] - sh_s[0, z, 0]
-                start = lax.shift_right_logical(first_row, 4) * 16
-                t_ref[0:WINDOW, :] = jnp.dot(
-                    src_ref[pl.ds(start, WINDOW), :], y_ref[pair], preferred_element_type=jnp.float32
-                ).astype(jnp.bfloat16)
-                top = top + jnp.dot(x_ref[pair, 0:128, :], t_ref[0:256, :], preferred_element_type=jnp.float32)
-                bottom = bottom + jnp.dot(
-                    x_ref[pair, 128:256, :], t_ref[128:384, :], preferred_element_type=jnp.float32
+        for z in range(PLANES):
+            first_row = HX - 1 + sh_s[slot, z, 0] - sh_s[0, z, 0]
+            start = lax.shift_right_logical(first_row, 4) * 16
+            t = jnp.dot(
+                src_ref[pl.ds(start, WINDOW), :], y_ref[slot * PLANES + z], preferred_element_type=jnp.float32
+            ).astype(jnp.bfloat16)
+            upper_ref[pl.ds(STRIP * z, STRIP), :] = t[0:STRIP]
+            lower_ref[pl.ds(STRIP * z, STRIP), :] = t[128 : 128 + STRIP]
+        for half, t_ref in enumerate((upper_ref, lower_ref)):
+            total = out_ref[pl.ds(128 * half, 128), :]
+            for g in range(PLANES // GROUP):
+                total = total + jnp.dot(
+                    x_ref[slot, half, g],
+                    t_ref[pl.ds(GROUP * STRIP * g, GROUP * STRIP), :],
+                    preferred_element_type=jnp.float32,
                 )
-            out_ref[0:128, :], out_ref[128:256, :] = top, bottom
-            return carry
-
-        lax.fori_loop(0, PLANES // len(t_refs), group, 0)
+            out_ref[pl.ds(128 * half, 128), :] = total
 
     def lanes(x):
         s = jnp.sum(x, axis=0, keepdims=True)
@@ -333,19 +341,23 @@
     h_ref[...] = jnp.zeros((TX, TY), jnp.float32)
 
     build(0)
+    build_rows(0)
     first.arrive(3, "a")
     first.arrive(1, "b")
     first.arrive(3, "b")
     first.arrive(1, "a")
     first.corners(0)
     build(3)
+    build_rows(3)
     first.corners(3)
     first.corners(1)
     first.arrive(2, "a")
     first.arrive(2, "b")
     build(1)
+    build_rows(1)
     first.corners(2)
     build(2)
+    build_rows(2)
     for slot in (0, 3, 1, 2):
         first.complete(slot)
         apply(e_refs[slot], q_ref, slot)
@@ -403,9 +415,9 @@
     q0 = q_ref[...]
     res_ref[0, 0] = meas_ref[0, 0] - alpha0 * q0 - alpha1 * (h_ref[...] + beta * q0)
     for slot in range(VIEWS):
-        for start in range(0, VROWS, 32):
-            rows = pl.ds(VX + start, 32)
-            yext_ref[slot, pl.ds(start, 32), :] = (
+        for start in range(0, VROWS, 16):
+            rows = pl.ds(VX + start, 16)
+            yext_ref[slot, pl.ds(start, 16), :] = (
                 weight0 * e_refs[slot][rows, :].astype(jnp.float32)
                 + alpha1 * r_refs[slot][rows, :].astype(jnp.float32)
             ).astype(jnp.bfloat16)
@@ -418,53 +430,54 @@
     sums2.finish()
 
 
-def volume_kernel(sh_s, tp_s, y_ref, res_in, vol_ref, res_out, b_ref, x_ref, t_ref):
+def volume_kernel(sh_s, tp_s, y_ref, res_in, vol_ref, res_out, b_ref, x_ref, upper_ref, lower_ref):
     view = lax.axis_index("view")
-    z = pl.program_id(0)
-
-    @pl.when(z == 0)
+    step = pl.program_id(0)
+
+    @pl.when(step == 0)
     def _():
         b_ref[...] = jnp.zeros(b_ref.shape, jnp.bfloat16)
-        x_ref[...] = jnp.zeros(x_ref.shape, jnp.bfloat16)
-        t_ref[...] = jnp.zeros(t_ref.shape, jnp.bfloat16)
         res_out[...] = res_in[...]
 
-    top = bottom = None
-    for v in range(VIEWS):
-        slot = lax.rem(v - view + VIEWS, VIEWS)
-        d = sh_s[slot, z, 1]
-        distance = (
-            lax.broadcasted_iota(jnp.int32, (224, 128), 0)
-            - lax.broadcasted_iota(jnp.int32, (224, 128), 1)
-            + (80 - HY)
-        )
-        value = jnp.where(
-            distance == d, tp_s[slot, z, 2], jnp.where(distance == d - 1, tp_s[slot, z, 3], 0.0)
-        ).astype(jnp.bfloat16)
-        b_ref[v, 80:304, 0:128] = value
-        b_ref[v, 208:432, 128:256] = value
-        first_row = HX - VX - 1 + sh_s[slot, z, 0]
-        start = pl.multiple_of(lax.shift_left(lax.shift_right_logical(first_row, 4), 4), 16)
-        m = first_row - start
-        b0, b1 = tp_s[slot, z, 0] * (PLANES**-0.5), tp_s[slot, z, 1] * (PLANES**-0.5)
-        for row_start, size, col_start in ((0, 128, 0), (96, 32, 128)):
+    for p in range(BACK_PLANES):
+        z = step * BACK_PLANES + p
+        rows = []
+        for v in range(VIEWS):
+            slot = lax.rem(v - view + VIEWS, VIEWS)
+            d = sh_s[slot, z, 1]
+            distance = (
+                lax.broadcasted_iota(jnp.int32, (224, 128), 0)
+                - lax.broadcasted_iota(jnp.int32, (224, 128), 1)
+                + (80 - HY)
+            )
+            value = jnp.where(
+                distance == d, tp_s[slot, z, 2], jnp.where(distance == d - 1, tp_s[slot, z, 3], 0.0)
+            ).astype(jnp.bfloat16)
+            pair = p * VIEWS + v
+            b_ref[pair, 80:304, 0:128] = value
+            b_ref[pair, 208:432, 128:256] = value
+            first_row = HX - VX - 1 + sh_s[slot, z, 0]
+            start = lax.shift_right_logical(first_row, 4) * 16
+            b0, b1 = tp_s[slot, z, 0] * (PLANES**-0.5), tp_s[slot, z, 1] * (PLANES**-0.5)
+            rows.append((first_row - start + STRIP * v, b0, b1))
+            t = jnp.dot(
+                y_ref[slot, pl.ds(start, BACK_WINDOW), :], b_ref[pair], preferred_element_type=jnp.float32
+            ).astype(jnp.bfloat16)
+            upper_ref[p, pl.ds(STRIP * v, STRIP), :] = t[0:STRIP]
+            lower_ref[p, pl.ds(STRIP * v, STRIP), :] = t[128 : 128 + STRIP]
+        for v, block, row_start, size in BAND:
+            m, b0, b1 = rows[v]
             distance = (
                 lax.broadcasted_iota(jnp.int32, (size, 128), 1)
                 - lax.broadcasted_iota(jnp.int32, (size, 128), 0)
-                + (col_start - row_start)
-            )
-            x_ref[v, pl.ds(row_start, size), pl.ds(col_start, 128)] = jnp.where(
+                + (128 * block - row_start)
+            )
+            x_ref[p, pl.ds(row_start, size), pl.ds(128 * block, 128)] = jnp.where(
                 distance == m, b1, jnp.where(distance == m + 1, b0, 0.0)
             ).astype(jnp.bfloat16)
-        t_ref[v, 0:BACK_WINDOW, :] = jnp.dot(
-            y_ref[slot, pl.ds(start, BACK_WINDOW), :], b_ref[v], preferred_element_type=jnp.float32
-        ).astype(jnp.bfloat16)
-        upper = jnp.dot(x_ref[v], t_ref[v, 0:256, :], preferred_element_type=jnp.float32)
-        lower = jnp.dot(x_ref[v], t_ref[v, 128:384, :], preferred_element_type=jnp.float32)
-        top = upper if top is None else top + upper
-        bottom = lower if bottom is None else bottom + lower
-    vol_ref[0, 0, 0:128, :] = top
-    vol_ref[0, 0, 128:256, :] = bottom
+    for p in range(BACK_PLANES):
+        vol_ref[0, p, 0:128, :] = jnp.dot(x_ref[p], upper_ref[p], preferred_element_type=jnp.float32)
+        vol_ref[0, p, 128:256, :] = jnp.dot(x_ref[p], lower_ref[p], preferred_element_type=jnp.float32)
 
 
 def local(grid_x, measured, shears, taps):
@@ -487,8 +500,9 @@
             [pltpu.VMEM((RX, RY), bf16)] * VIEWS,
             [pltpu.VMEM((RX, RY), bf16)] * VIEWS,
             pltpu.VMEM((VIEWS * PLANES, RY, TY), bf16),
-            pltpu.VMEM((VIEWS * PLANES, TX, 256), bf16),
-            [pltpu.VMEM((T_ROWS, TY), bf16)] * 4,
+            pltpu.VMEM((VIEWS, 2, PLANES // GROUP, 128, GROUP * STRIP), bf16),
+            pltpu.VMEM((PLANES * STRIP, TY), bf16),
+            pltpu.VMEM((PLANES * STRIP, TY), bf16),
             pltpu.VMEM((TX, TY), f32),
             pltpu.VMEM((TX, TY), f32),
             pltpu.VMEM((VIEWS, PLANES, 128), jnp.int32),
@@ -511,20 +525,21 @@
     volume, residual = pl.pallas_call(
         volume_kernel,
         name="back_project",
-        grid=(PLANES,),
+        grid=(PLANES // BACK_PLANES,),
         out_shape=(
             jax.ShapeDtypeStruct((1, PLANES, TX, TY), f32),
             jax.ShapeDtypeStruct((1, 1, TX, TY), f32),
         ),
         in_specs=[smem, smem, vmem, vmem],
         out_specs=(
-            pl.BlockSpec((1, 1, TX, TY), lambda z: (0, z, 0, 0)),
+            pl.BlockSpec((1, BACK_PLANES, TX, TY), lambda z: (0, z, 0, 0)),
             pl.BlockSpec((1, 1, TX, TY), lambda z: (0, 0, 0, 0)),
         ),
         scratch_shapes=[
-            pltpu.VMEM((VIEWS, RY, TY), bf16),
-            pltpu.VMEM((VIEWS, 128, 256), bf16),
-            pltpu.VMEM((VIEWS, T_ROWS, TY), bf16),
+            pltpu.VMEM((BACK_PLANES * VIEWS, RY, TY), bf16),
+            pltpu.VMEM((BACK_PLANES, 128, VIEWS * STRIP), bf16),
+            pltpu.VMEM((BACK_PLANES, VIEWS * STRIP, TY), bf16),
+            pltpu.VMEM((BACK_PLANES, VIEWS * STRIP, TY), bf16),
         ],
         compiler_params=pltpu.CompilerParams(vmem_limit_bytes=32 * 1024 * 1024),
     )(sh_all, tp_all, yext, partial)

time: 115 us -> 87.7 us (0.76)
  Pallas kernels: 112 us -> 84.4 us
    pallas_call x1, Pallas kernels: 90.2 us -> 73.6 us  [local(): pl.pallas_call(functools.partial(solve_kernel, grid_x), name='solve', out...]
    pallas_call x1, Pallas kernels: 21.4 us -> 10.9 us  [local(): pl.pallas_call(volume_kernel, name='back_project', grid=(PLANES // BACK_P...]
where the time goes in v2:
time: 87.7 us; the launch traced here: 87.5 us
  Pallas kernels  84.4 us (96%)
  local copies, waits for them, and re-layouts  2.47 us (3%)
    pallas_call x1, Pallas kernels, local(): pl.pallas_call(functools.partial(solve_kernel, grid_x), name='solve', out...  73.6 us
    pallas_call x1, Pallas kernels, local(): pl.pallas_call(volume_kernel, name='back_project', grid=(PLANES // BACK_P...  10.9 us
    unnamed x4, local copies, waits for them, and re-layouts  2.47 us

profile of v2, /device:TPU:1, one launch (start us, length us, event | category | flops | bytes accessed | tf_op | source)
XLA Modules:
  0.0 87.5 jit_solution(14640752345080582363)
XLA Ops:
  0.6 0.8 copy.6.tp_ref
  1.4 0.8 copy.5.sh_ref
  2.2 0.0 copy-start
  2.2 0.9 %copy-done = f32[1,1,256,256]{3,2,1,0:T(8,128)S(1)} copy-done((f32[1,1,256,256]{3,2,1,0:T(8,128)S(1)}, f32[1,1,256,256]{3,2,1,0:T(8,128)}, u32[]{:S(2)}) %copy-start) | copy-done | bytes 262168
  3.1 73.6 %solve.1 = (bf16[4,368,512]{2,1,0:T(8,128)(2,1)S(1)}, f32[1,1,256,256]{3,2,1,0:T(8,128)S(1)}, s32[4,16,128]{2,1,0:T(8,128)S(1)}, f32[4,16,128]{2,1,0:T(8,128)S(1)}) custom-call(f32[1,1,256,256]{3,2,1,0:T(8,128)S(1)} %copy-done, s32[1,16,2]{2,1,0:T(8,128)S(1)} %copy.5.sh_ref, bf16[1,16,4]{2,1,0:T(8,128)(2,1)S(1)} %copy.6.tp_ref), custom_call_target="tpu_custom_call" | custom-call | tf_op jit(solution)/shard_map/solve/pallas_call | solution.py:487
  76.7 10.9 %back_project.1 = (f32[1,16,256,256]{3,2,1,0:T(8,128)}, f32[1,1,256,256]{3,2,1,0:T(8,128)}) custom-call(s32[4,16,128]{2,1,0:T(8,128)S(1)} %get-tuple-element.6.sh_s, f32[4,16,128]{2,1,0:T(8,128)S(1)} %get-tuple-element.7.tp_s, bf16[4,368,512]{2,1,0:T(8,128)(2,1)S(1)} %get-tuple-element.8.y_ref, f32[1,1,256,256]{3,2,1,0:T(8,128)S(1)} %get-tuple-element.9.res_in), custom_call_target="tpu_custom_call" | custom-call | tf_op jit(solution)/shard_map/back_project/pallas_call | solution.py:525
Async XLA Ops:
  2.2 0.9 %copy-start = (f32[1,1,256,256]{3,2,1,0:T(8,128)S(1)}, f32[1,1,256,256]{3,2,1,0:T(8,128)}, u32[]{:S(2)}) copy-start(f32[1,1,256,256]{3,2,1,0:T(8,128)} %meas_ref.1) | copy-start | bytes 786436

commit v3 on v2

--- a/solution.py
+++ b/solution.py
@@ -16,12 +16,8 @@
 HY = 128
 RX = TX + 2 * HX
 RY = TY + 2 * HY
-VX = 48
-VROWS = RX - VX - 32
 WINDOW = 288
-BACK_WINDOW = 288
 STRIP = 160
-BACK_PLANES = 4
 GROUP = 4
 BAND = (
     (0, 0, 0, 128), (0, 1, 96, 32), (1, 1, 0, 96), (1, 2, 64, 64),
@@ -46,10 +42,10 @@
 
 def solve_kernel(
     grid_x,
-    meas_ref, sh_ref, tp_ref,
-    yext_ref, res_ref, sh_s, tp_s,
-    e_refs, f_refs, r_refs, y_ref, x_ref, upper_ref, lower_ref, q_ref, h_ref,
-    sh_v, tp_v, ra_ref, rb_ref, rc_ref,
+    meas_hbm, sh_ref, tp_ref,
+    vol_ref, res_ref,
+    meas_ref, e_refs, f_refs, y_ref, x_ref, upper_ref, lower_ref, q_ref, p_ref, back_ref, by_ref, bx_ref, strip_refs,
+    sh_v, tp_v, sh_s, tp_s, ra_ref, rb_ref, rc_ref,
     send_sems, recv_sems, p_send, p_recv, p_local, a_send, a_recv,
 ):
     tile = lax.axis_index("tile")
@@ -78,11 +74,14 @@
     for partner in partners:
         pl.semaphore_signal(barrier, inc=1, device_id=partner, device_id_type=MESH)
 
-    e_refs[0][pl.ds(HX, TX), pl.ds(HY, TY)] = meas_ref[0, 0].astype(jnp.bfloat16)
-    sh_v[0] = jnp.zeros((PLANES, 128), jnp.int32)
-    sh_v[0, :, 0:2] = sh_ref[0]
-    tp_v[0] = jnp.zeros((PLANES, 128), jnp.float32)
-    tp_v[0, :, 0:4] = tp_ref[0].astype(jnp.float32)
+    loading = pltpu.make_async_copy(meas_hbm.at[0, 0], meas_ref, p_local.at[2])
+    loading.start()
+    sh_v[0] = jnp.zeros((8, 128), jnp.int32)
+    sh_v[0, 0:2, 0:PLANES] = sh_ref[0]
+    tp_v[0] = jnp.zeros((8, 128), jnp.float32)
+    tp_v[0, 0:4, 0:PLANES] = tp_ref[0].astype(jnp.float32)
+    loading.wait()
+    e_refs[0][pl.ds(HX, TX), pl.ds(HY, TY)] = meas_ref[...].astype(jnp.bfloat16)
 
     pl.semaphore_wait(barrier, len(partners))
 
@@ -216,10 +215,10 @@
 
     def build(slot):
         def one(z, carry):
-            shear = sh_s[0, z, 1]
-            d = sh_s[slot, z, 1] - shear
-            a0, a1 = tp_s[0, z, 2], tp_s[0, z, 3]
-            b0, b1 = tp_s[slot, z, 2], tp_s[slot, z, 3]
+            shear = sh_s[0, 1, z]
+            d = sh_s[slot, 1, z] - shear
+            a0, a1 = tp_s[0, 2, z], tp_s[0, 3, z]
+            b0, b1 = tp_s[slot, 2, z], tp_s[slot, 3, z]
             col = lax.broadcasted_iota(jnp.int32, (1, 128), 1)
             distance = (
                 lax.broadcasted_iota(jnp.int32, (320, 128), 0)
@@ -248,11 +247,11 @@
             scalars = []
             for u in range(GROUP):
                 z = GROUP * g + u
-                shear = sh_s[0, z, 0]
-                first_row = HX - 1 + sh_s[slot, z, 0] - shear
+                shear = sh_s[0, 0, z]
+                first_row = HX - 1 + sh_s[slot, 0, z] - shear
                 m = first_row - lax.shift_right_logical(first_row, 4) * 16 + STRIP * u
-                a0, a1 = tp_s[0, z, 0] * (1.0 / PLANES), tp_s[0, z, 1] * (1.0 / PLANES)
-                b0, b1 = tp_s[slot, z, 0], tp_s[slot, z, 1]
+                a0, a1 = tp_s[0, 0, z] * (1.0 / PLANES), tp_s[0, 1, z] * (1.0 / PLANES)
+                b0, b1 = tp_s[slot, 0, z], tp_s[slot, 1, z]
                 scalars.append((m, a0 * b1, a0 * b0, a1 * b1, a1 * b0, shear + row_low, shear + row_high))
             for u, block, row_start, size in BAND:
                 m, am, az, bz, bp, low, high = scalars[u]
@@ -274,7 +273,7 @@
 
     def apply(src_ref, out_ref, slot):
         for z in range(PLANES):
-            first_row = HX - 1 + sh_s[slot, z, 0] - sh_s[0, z, 0]
+            first_row = HX - 1 + sh_s[slot, 0, z] - sh_s[0, 0, z]
             start = lax.shift_right_logical(first_row, 4) * 16
             t = jnp.dot(
                 src_ref[pl.ds(start, WINDOW), :], y_ref[slot * PLANES + z], preferred_element_type=jnp.float32
@@ -296,8 +295,7 @@
         return s[:, 0:128] + s[:, 128:256]
 
     class Sum:
-        def __init__(self, which, rows):
-            self.which = which
+        def __init__(self, rows):
             self.stages = (
                 (ra_ref, view, VIEWS, to_view, 0),
                 (rb_ref, gy, GRID_Y, to_col, VIEWS),
@@ -309,12 +307,12 @@
 
         def send(self, stage):
             ref, me, size, to, base = self.stages[stage]
-            ref[self.which, me] = self.value
+            ref[me] = self.value
             self.current = []
-            for step in range(1, size):
+            for step in sorted(range(1, size), key=lambda k: -min(k, size - k)):
                 copy = pltpu.make_async_remote_copy(
-                    src_ref=ref.at[self.which, me], dst_ref=ref.at[self.which, me],
-                    send_sem=a_send.at[self.which, base + step], recv_sem=a_recv.at[self.which, base + step],
+                    src_ref=ref.at[me], dst_ref=ref.at[me],
+                    send_sem=a_send.at[base + step], recv_sem=a_recv.at[base + step],
                     device_id=to(step), device_id_type=MESH,
                 )
                 copy.start()
@@ -325,9 +323,9 @@
             ref, me, size, to, base = self.stages[stage]
             for copy in self.current:
                 copy.wait_recv()
-            total = ref[self.which, 0]
+            total = ref[0]
             for i in range(1, size):
-                total = total + ref[self.which, i]
+                total = total + ref[i]
             self.value = total
 
         def row(self, i):
@@ -337,22 +335,66 @@
             for copy in self.copies:
                 copy.wait_send()
 
+    by_ref[...] = jnp.zeros(by_ref.shape, jnp.bfloat16)
+
+    def back(chunk):
+        for u in range(GROUP):
+            z = GROUP * chunk + u
+            for slot in range(VIEWS):
+                place = lax.rem(view + slot, VIEWS)
+                d = sh_s[slot, 1, z]
+                distance = (
+                    lax.broadcasted_iota(jnp.int32, (224, 128), 0)
+                    - lax.broadcasted_iota(jnp.int32, (224, 128), 1)
+                    + (80 - HY)
+                )
+                value = jnp.where(
+                    distance == d, tp_s[slot, 2, z], jnp.where(distance == d - 1, tp_s[slot, 3, z], 0.0)
+                ).astype(jnp.bfloat16)
+                pair = VIEWS * u + slot
+                by_ref[pair, 80:304, 0:128] = value
+                by_ref[pair, 208:432, 128:256] = value
+                start = lax.shift_right_logical(HX - 1 + sh_s[slot, 0, z], 4) * 16
+                both = jnp.concatenate(
+                    [e_refs[slot][pl.ds(start, WINDOW), :], f_refs[slot][pl.ds(start, WINDOW), :]], axis=0
+                )
+                t = jnp.dot(both, by_ref[pair], preferred_element_type=jnp.float32).astype(jnp.bfloat16)
+                for k, first in enumerate((0, 128, WINDOW, WINDOW + 128)):
+                    strip_refs[k][u, pl.ds(STRIP * place, STRIP), :] = t[first : first + STRIP]
+            for v, block, row_start, size in BAND:
+                slot = lax.rem(v - view + VIEWS, VIEWS)
+                first_row = HX - 1 + sh_s[slot, 0, z]
+                m = first_row - lax.shift_right_logical(first_row, 4) * 16 + STRIP * v
+                b0, b1 = tp_s[slot, 0, z] * (PLANES**-0.5), tp_s[slot, 1, z] * (PLANES**-0.5)
+                distance = (
+                    lax.broadcasted_iota(jnp.int32, (size, 128), 1)
+                    - lax.broadcasted_iota(jnp.int32, (size, 128), 0)
+                    + (128 * block - row_start)
+                )
+                bx_ref[u, pl.ds(row_start, size), pl.ds(128 * block, 128)] = jnp.where(
+                    distance == m, b1, jnp.where(distance == m + 1, b0, 0.0)
+                ).astype(jnp.bfloat16)
+        for u in range(GROUP):
+            z = GROUP * chunk + u
+            for k, (ref, first) in enumerate(((vol_ref, 0), (vol_ref, 128), (back_ref, 0), (back_ref, 128))):
+                ref[0, z, pl.ds(first, 128), :] = jnp.dot(
+                    bx_ref[u], strip_refs[k][u], preferred_element_type=jnp.float32
+                )
+
     q_ref[...] = jnp.zeros((TX, TY), jnp.float32)
-    h_ref[...] = jnp.zeros((TX, TY), jnp.float32)
+    p_ref[...] = jnp.zeros((TX, TY), jnp.float32)
 
     build(0)
     build_rows(0)
-    first.arrive(3, "a")
-    first.arrive(1, "b")
-    first.arrive(3, "b")
-    first.arrive(1, "a")
+    for slot, part in ((3, "a"), (1, "b"), (3, "b"), (1, "a")):
+        first.arrive(slot, part)
     first.corners(0)
     build(3)
     build_rows(3)
+    first.arrive(2, "a")
+    first.arrive(2, "b")
     first.corners(3)
     first.corners(1)
-    first.arrive(2, "a")
-    first.arrive(2, "b")
     build(1)
     build_rows(1)
     first.corners(2)
@@ -365,138 +407,70 @@
     second = Exchange(f_refs, 1)
     f_refs[0][pl.ds(HX, TX), pl.ds(HY, TY)] = q_ref[...].astype(jnp.bfloat16)
     second.begin()
-    q0 = q_ref[...]
-    r0 = e_refs[0][pl.ds(HX, TX), pl.ds(HY, TY)].astype(jnp.float32)
-    sums = Sum(0, [lanes(r0 * q0), lanes(q0 * q0)])
-    sums.send(0)
-    sums.receive(0)
-    sums.send(1)
-    second.arrive(3, "a")
-    second.arrive(1, "b")
-    second.arrive(3, "b")
-    second.arrive(1, "a")
     second.corners(0)
-    sums.receive(1)
-    sums.send(2)
+    for slot, part in ((3, "a"), (1, "b"), (3, "b"), (1, "a")):
+        second.arrive(slot, part)
+    second.complete(0)
+    apply(f_refs[0], p_ref, 0)
+    second.arrive(2, "a")
+    second.arrive(2, "b")
     second.corners(3)
     second.corners(1)
-    second.arrive(2, "a")
-    second.arrive(2, "b")
-    sums.receive(2)
-    gamma0, norm0 = sums.row(0), sums.row(1)
-    alpha0 = gamma0 / (norm0 + TINY)
     second.corners(2)
-
-    def update(slot):
-        for start in range(0, RX, 64):
-            rows = pl.ds(start, 64)
-            r_refs[slot][rows, :] = (
-                e_refs[slot][rows, :].astype(jnp.float32) - alpha0 * f_refs[slot][rows, :].astype(jnp.float32)
-            ).astype(jnp.bfloat16)
-
-    for slot in (0, 3, 1, 2):
+    for slot in (3, 1, 2):
         second.complete(slot)
-        update(slot)
-        apply(r_refs[slot], h_ref, slot)
-
-    h1 = h_ref[...]
-    q0 = q_ref[...]
-    r1 = r_refs[0][pl.ds(HX, TX), pl.ds(HY, TY)].astype(jnp.float32)
-    sums2 = Sum(1, [lanes(r1 * h1), lanes(h1 * h1), lanes(h1 * q0)])
+        apply(f_refs[slot], p_ref, slot)
+
+    r0 = e_refs[0][pl.ds(HX, TX), pl.ds(HY, TY)].astype(jnp.float32)
+    q0, p = q_ref[...], p_ref[...]
+    sums = Sum([lanes(r0 * q0), lanes(q0 * q0), lanes(r0 * p), lanes(q0 * p), lanes(p * p)])
     for stage in range(3):
-        sums2.send(stage)
-        sums2.receive(stage)
-    gamma1 = sums2.row(0)
+        sums.send(stage)
+        back(stage)
+        sums.receive(stage)
+    back(3)
+    r0q0, q0q0, r0p, q0p, pp = [sums.row(i) for i in range(5)]
+    gamma0 = r0q0
+    alpha0 = gamma0 / (q0q0 + TINY)
+    gamma1 = r0q0 - alpha0 * (r0p + q0q0) + alpha0 * alpha0 * q0p
     beta = gamma1 / (gamma0 + TINY)
-    norm1 = sums2.row(1) + 2.0 * beta * sums2.row(2) + beta * beta * norm0
-    alpha1 = gamma1 / (norm1 + TINY)
-    weight0 = alpha0 + alpha1 * beta
-
-    q0 = q_ref[...]
-    res_ref[0, 0] = meas_ref[0, 0] - alpha0 * q0 - alpha1 * (h_ref[...] + beta * q0)
-    for slot in range(VIEWS):
-        for start in range(0, VROWS, 16):
-            rows = pl.ds(VX + start, 16)
-            yext_ref[slot, pl.ds(start, 16), :] = (
-                weight0 * e_refs[slot][rows, :].astype(jnp.float32)
-                + alpha1 * r_refs[slot][rows, :].astype(jnp.float32)
-            ).astype(jnp.bfloat16)
+    h1h1 = q0q0 - 2.0 * alpha0 * q0p + alpha0 * alpha0 * pp
+    h1q0 = q0q0 - alpha0 * q0p
+    alpha1 = gamma1 / (h1h1 + 2.0 * beta * h1q0 + beta * beta * q0q0 + TINY)
+
+    weight0 = alpha0 + alpha1 * beta + alpha1
+    weight1 = alpha1 * alpha0
+
+    def combine(z, carry):
+        vol_ref[0, z] = weight0 * vol_ref[0, z] - weight1 * back_ref[0, z]
+        return carry
+
+    lax.fori_loop(0, PLANES, combine, 0)
+    q0, p = q_ref[...], p_ref[...]
+    res_ref[0, 0] = meas_ref[...] - alpha0 * q0 - alpha1 * ((q0 - alpha0 * p) + beta * q0)
 
     for copy in parameter_copies:
         copy.wait_send()
     first.finish()
     second.finish()
     sums.finish()
-    sums2.finish()
-
-
-def volume_kernel(sh_s, tp_s, y_ref, res_in, vol_ref, res_out, b_ref, x_ref, upper_ref, lower_ref):
-    view = lax.axis_index("view")
-    step = pl.program_id(0)
-
-    @pl.when(step == 0)
-    def _():
-        b_ref[...] = jnp.zeros(b_ref.shape, jnp.bfloat16)
-        res_out[...] = res_in[...]
-
-    for p in range(BACK_PLANES):
-        z = step * BACK_PLANES + p
-        rows = []
-        for v in range(VIEWS):
-            slot = lax.rem(v - view + VIEWS, VIEWS)
-            d = sh_s[slot, z, 1]
-            distance = (
-                lax.broadcasted_iota(jnp.int32, (224, 128), 0)
-                - lax.broadcasted_iota(jnp.int32, (224, 128), 1)
-                + (80 - HY)
-            )
-            value = jnp.where(
-                distance == d, tp_s[slot, z, 2], jnp.where(distance == d - 1, tp_s[slot, z, 3], 0.0)
-            ).astype(jnp.bfloat16)
-            pair = p * VIEWS + v
-            b_ref[pair, 80:304, 0:128] = value
-            b_ref[pair, 208:432, 128:256] = value
-            first_row = HX - VX - 1 + sh_s[slot, z, 0]
-            start = lax.shift_right_logical(first_row, 4) * 16
-            b0, b1 = tp_s[slot, z, 0] * (PLANES**-0.5), tp_s[slot, z, 1] * (PLANES**-0.5)
-            rows.append((first_row - start + STRIP * v, b0, b1))
-            t = jnp.dot(
-                y_ref[slot, pl.ds(start, BACK_WINDOW), :], b_ref[pair], preferred_element_type=jnp.float32
-            ).astype(jnp.bfloat16)
-            upper_ref[p, pl.ds(STRIP * v, STRIP), :] = t[0:STRIP]
-            lower_ref[p, pl.ds(STRIP * v, STRIP), :] = t[128 : 128 + STRIP]
-        for v, block, row_start, size in BAND:
-            m, b0, b1 = rows[v]
-            distance = (
-                lax.broadcasted_iota(jnp.int32, (size, 128), 1)
-                - lax.broadcasted_iota(jnp.int32, (size, 128), 0)
-                + (128 * block - row_start)
-            )
-            x_ref[p, pl.ds(row_start, size), pl.ds(128 * block, 128)] = jnp.where(
-                distance == m, b1, jnp.where(distance == m + 1, b0, 0.0)
-            ).astype(jnp.bfloat16)
-    for p in range(BACK_PLANES):
-        vol_ref[0, p, 0:128, :] = jnp.dot(x_ref[p], upper_ref[p], preferred_element_type=jnp.float32)
-        vol_ref[0, p, 128:256, :] = jnp.dot(x_ref[p], lower_ref[p], preferred_element_type=jnp.float32)
 
 
 def local(grid_x, measured, shears, taps):
     f32, bf16 = jnp.float32, jnp.bfloat16
     vmem = pl.BlockSpec(memory_space=pltpu.VMEM)
-    smem = pl.BlockSpec(memory_space=pltpu.SMEM)
-    yext, partial, sh_all, tp_all = pl.pallas_call(
+    partners = VIEWS + GRID_Y + grid_x
+    return pl.pallas_call(
         functools.partial(solve_kernel, grid_x),
         name="solve",
         out_shape=(
-            jax.ShapeDtypeStruct((VIEWS, VROWS, RY), bf16),
+            jax.ShapeDtypeStruct((1, PLANES, TX, TY), f32),
             jax.ShapeDtypeStruct((1, 1, TX, TY), f32),
-            jax.ShapeDtypeStruct((VIEWS, PLANES, 128), jnp.int32),
-            jax.ShapeDtypeStruct((VIEWS, PLANES, 128), f32),
         ),
-        in_specs=[vmem, vmem, vmem],
-        out_specs=(vmem, vmem, smem, smem),
+        in_specs=[pl.BlockSpec(memory_space=pl.ANY), vmem, vmem],
+        out_specs=(vmem, vmem),
         scratch_shapes=[
-            [pltpu.VMEM((RX, RY), bf16)] * VIEWS,
+            pltpu.VMEM((TX, TY), f32),
             [pltpu.VMEM((RX, RY), bf16)] * VIEWS,
             [pltpu.VMEM((RX, RY), bf16)] * VIEWS,
             pltpu.VMEM((VIEWS * PLANES, RY, TY), bf16),
@@ -505,45 +479,29 @@
             pltpu.VMEM((PLANES * STRIP, TY), bf16),
             pltpu.VMEM((TX, TY), f32),
             pltpu.VMEM((TX, TY), f32),
-            pltpu.VMEM((VIEWS, PLANES, 128), jnp.int32),
-            pltpu.VMEM((VIEWS, PLANES, 128), f32),
-            pltpu.VMEM((2, VIEWS, 8, 128), f32),
-            pltpu.VMEM((2, GRID_Y, 8, 128), f32),
-            pltpu.VMEM((2, grid_x, 8, 128), f32),
+            pltpu.VMEM((1, PLANES, TX, TY), f32),
+            pltpu.VMEM((GROUP * VIEWS, RY, TY), bf16),
+            pltpu.VMEM((GROUP, 128, VIEWS * STRIP), bf16),
+            [pltpu.VMEM((GROUP, VIEWS * STRIP, TY), bf16)] * 4,
+            pltpu.VMEM((VIEWS, 8, 128), jnp.int32),
+            pltpu.VMEM((VIEWS, 8, 128), f32),
+            pltpu.SMEM((VIEWS, 8, 128), jnp.int32),
+            pltpu.SMEM((VIEWS, 8, 128), f32),
+            pltpu.VMEM((VIEWS, 8, 128), f32),
+            pltpu.VMEM((GRID_Y, 8, 128), f32),
+            pltpu.VMEM((grid_x, 8, 128), f32),
             pltpu.SemaphoreType.DMA((2, N_SEMS)),
             pltpu.SemaphoreType.DMA((2, N_SEMS)),
             pltpu.SemaphoreType.DMA((2, VIEWS)),
             pltpu.SemaphoreType.DMA((2, VIEWS)),
-            pltpu.SemaphoreType.DMA((2,)),
-            pltpu.SemaphoreType.DMA((2, VIEWS + GRID_Y + grid_x)),
-            pltpu.SemaphoreType.DMA((2, VIEWS + GRID_Y + grid_x)),
+            pltpu.SemaphoreType.DMA((3,)),
+            pltpu.SemaphoreType.DMA((partners,)),
+            pltpu.SemaphoreType.DMA((partners,)),
         ],
         compiler_params=pltpu.CompilerParams(
-            collective_id=0, has_side_effects=True, vmem_limit_bytes=48 * 1024 * 1024
+            collective_id=0, has_side_effects=True, vmem_limit_bytes=50 * 1024 * 1024
         ),
-    )(measured, shears, taps)
-    volume, residual = pl.pallas_call(
-        volume_kernel,
-        name="back_project",
-        grid=(PLANES // BACK_PLANES,),
-        out_shape=(
-            jax.ShapeDtypeStruct((1, PLANES, TX, TY), f32),
-            jax.ShapeDtypeStruct((1, 1, TX, TY), f32),
-        ),
-        in_specs=[smem, smem, vmem, vmem],
-        out_specs=(
-            pl.BlockSpec((1, BACK_PLANES, TX, TY), lambda z: (0, z, 0, 0)),
-            pl.BlockSpec((1, 1, TX, TY), lambda z: (0, 0, 0, 0)),
-        ),
-        scratch_shapes=[
-            pltpu.VMEM((BACK_PLANES * VIEWS, RY, TY), bf16),
-            pltpu.VMEM((BACK_PLANES, 128, VIEWS * STRIP), bf16),
-            pltpu.VMEM((BACK_PLANES, VIEWS * STRIP, TY), bf16),
-            pltpu.VMEM((BACK_PLANES, VIEWS * STRIP, TY), bf16),
-        ],
-        compiler_params=pltpu.CompilerParams(vmem_limit_bytes=32 * 1024 * 1024),
-    )(sh_all, tp_all, yext, partial)
-    return volume, residual
+    )(measured, jnp.transpose(shears, (0, 2, 1)), jnp.transpose(taps, (0, 2, 1)))
 
 
 def solution(mesh):

time: 87.7 us -> 82.4 us (0.940)
  Pallas kernels: 84.4 us -> 73.9 us
  local copies, waits for them, and re-layouts: 2.47 us -> 7.6 us
    pallas_call x1 -> x0, Pallas kernels: 10.9 us -> none  [local(): pl.pallas_call(volume_kernel, name='back_project', grid=(PLANES // BACK_P...]
    unnamed x4 -> x8, local copies, waits for them, and re-layouts: 2.47 us -> 7.6 us
where the time goes in v3:
time: 82.4 us; the launch traced here: 82.2 us
  Pallas kernels  73.9 us (90%)
  local copies, waits for them, and re-layouts  7.6 us (9%)
    pallas_call x1, Pallas kernels, local(): pl.pallas_call(functools.partial(solve_kernel, grid_x), name='solve', out...  73.9 us
    unnamed x8, local copies, waits for them, and re-layouts  7.6 us

profile of v3, /device:TPU:1, one launch (start us, length us, event | category | flops | bytes accessed | tf_op | source)
XLA Modules:
  0.0 82.2 jit_solution(2499615230809405161)
XLA Ops:
  0.6 0.0 copy-start
  0.6 0.9 %copy-done = f32[1,1,256,256]{3,2,1,0:T(8,128)S(1)} copy-done((f32[1,1,256,256]{3,2,1,0:T(8,128)S(1)}, f32[1,1,256,256]{3,2,1,0:T(8,128)}, u32[]{:S(2)}) %copy-start) | copy-done | bytes 262168
  1.6 0.0 copy-start.1
  1.6 0.7 copy-done.1
  2.3 0.0 copy-start.2
  2.3 0.7 copy-done.2
  2.9 73.9 %solve.1 = (f32[1,16,256,256]{3,2,1,0:T(8,128)}, f32[1,1,256,256]{3,2,1,0:T(8,128)S(1)}) custom-call(f32[1,1,256,256]{3,2,1,0:T(8,128)S(1)} %copy-done, s32[1,2,16]{2,1,0:T(2,128)S(1)} %bitcast.2, bf16[1,4,16]{2,1,0:T(4,128)(2,1)S(1)} %bitcast.3), custom_call_target="tpu_custom_call" | custom-call | tf_op jit(solution)/shard_map/solve/pallas_call | solution.py:463
  76.9 4.6 %copy.7 = f32[1,16,256,256]{3,2,1,0:T(8,128)} copy(f32[1,16,256,256]{3,2,1,0:T(8,128)} %get-tuple-element.4) | data formatting | bytes 8388608
  81.5 0.7 copy.8
Async XLA Ops:
  0.6 1.0 %copy-start = (f32[1,1,256,256]{3,2,1,0:T(8,128)S(1)}, f32[1,1,256,256]{3,2,1,0:T(8,128)}, u32[]{:S(2)}) copy-start(f32[1,1,256,256]{3,2,1,0:T(8,128)} %meas_hbm.1) | copy-start | bytes 786436
  1.6 0.7 copy-start.1
  2.3 0.7 copy-start.2

commit v4 on v3

--- a/solution.py
+++ b/solution.py
@@ -42,9 +42,9 @@
 
 def solve_kernel(
     grid_x,
-    meas_hbm, sh_ref, tp_ref,
+    meas_hbm, sh_hbm, tp_hbm,
     vol_ref, res_ref,
-    meas_ref, e_refs, f_refs, y_ref, x_ref, upper_ref, lower_ref, q_ref, p_ref, back_ref, by_ref, bx_ref, strip_refs,
+    meas_ref, sh_ref, tp_ref, e_refs, f_refs, y_ref, x_ref, q_ref, p_ref, back_refs, by_ref, bx_ref, strip_refs,
     sh_v, tp_v, sh_s, tp_s, ra_ref, rb_ref, rc_ref,
     send_sems, recv_sems, p_send, p_recv, p_local, a_send, a_recv,
 ):
@@ -74,16 +74,117 @@
     for partner in partners:
         pl.semaphore_signal(barrier, inc=1, device_id=partner, device_id_type=MESH)
 
-    loading = pltpu.make_async_copy(meas_hbm.at[0, 0], meas_ref, p_local.at[2])
-    loading.start()
+    loading = [
+        pltpu.make_async_copy(src.at[0], dst, p_local.at[k])
+        for k, (src, dst) in enumerate(((meas_hbm.at[0], meas_ref), (sh_hbm, sh_ref), (tp_hbm, tp_ref)))
+    ]
+    for copy in loading:
+        copy.start()
+    for copy in loading:
+        copy.wait()
+    e_refs[0][pl.ds(HX, TX), pl.ds(HY, TY)] = meas_ref[...].astype(jnp.bfloat16)
     sh_v[0] = jnp.zeros((8, 128), jnp.int32)
-    sh_v[0, 0:2, 0:PLANES] = sh_ref[0]
+    sh_v[0, 0:2, 0:PLANES] = sh_ref[...]
     tp_v[0] = jnp.zeros((8, 128), jnp.float32)
-    tp_v[0, 0:4, 0:PLANES] = tp_ref[0].astype(jnp.float32)
-    loading.wait()
-    e_refs[0][pl.ds(HX, TX), pl.ds(HY, TY)] = meas_ref[...].astype(jnp.bfloat16)
+    tp_v[0, 0:4, 0:PLANES] = tp_ref[...].astype(jnp.float32)
 
     pl.semaphore_wait(barrier, len(partners))
+
+    class Exchange:
+        def __init__(self, bufs, which):
+            self.bufs, self.which, self.copies = bufs, which, {}
+
+        def send(self, key, sem, src, dst, device):
+            copy = pltpu.make_async_remote_copy(
+                src_ref=src, dst_ref=dst,
+                send_sem=send_sems.at[self.which, sem], recv_sem=recv_sems.at[self.which, sem],
+                device_id=device, device_id_type=MESH,
+            )
+            copy.start()
+            self.copies[key] = copy
+
+        def region(self, slot, rows, cols):
+            return self.bufs[slot].at[pl.ds(*rows), pl.ds(*cols)]
+
+        def along_view(self, src_slot, dst_slot, part, sem, step):
+            rows = PARTS[part]
+            self.send(
+                ("x", dst_slot, part), sem,
+                self.region(src_slot, rows, (HY, TY)), self.region(dst_slot, rows, (HY, TY)),
+                to_view(step),
+            )
+
+        def along_views(self):
+            self.along_view(0, 3, "a", 0, 1)
+            self.along_view(0, 1, "b", 1, -1)
+            self.along_view(0, 3, "b", 2, 1)
+            self.along_view(0, 1, "a", 3, -1)
+
+        def own(self):
+            self.spread(0, "a")
+            self.spread(0, "b")
+
+        def columns(self, slot, part):
+            rows = PARTS[part]
+            sem = Y_BASE + 8 * slot + 2 * PART_ID[part]
+            self.send(
+                ("y", slot, part, 0), sem,
+                self.region(slot, rows, (HY, HY)), self.region(slot, rows, (HY + TY, HY)), to_col(-1),
+            )
+            self.send(
+                ("y", slot, part, 1), sem + 1,
+                self.region(slot, rows, (TY, HY)), self.region(slot, rows, (0, HY)), to_col(1),
+            )
+
+        def spread(self, slot, part):
+            if part == "a":
+                self.send(
+                    ("z", slot, "bottom"), Z_BASE + 2 * slot,
+                    self.region(slot, (HX, HX), (HY, TY)),
+                    self.region(slot, (HX + TX, HX), (HY, TY)), to_row(-1),
+                )
+            else:
+                self.send(
+                    ("z", slot, "top"), Z_BASE + 2 * slot + 1,
+                    self.region(slot, (TX, HX), (HY, TY)),
+                    self.region(slot, (0, HX), (HY, TY)), to_row(1),
+                )
+            self.columns(slot, part)
+
+        def arrive(self, slot, part):
+            self.copies["x", slot, part].wait_recv()
+            if slot == 3 and part == "a":
+                self.along_view(3, 2, "a", 4, 1)
+            if slot == 1 and part == "b":
+                self.along_view(1, 2, "b", 5, -1)
+            self.spread(slot, part)
+
+        def corners(self, slot):
+            for part, edge in (("top", 0), ("bottom", grid_x - 1)):
+                self.copies["z", slot, part].wait_recv()
+
+                @pl.when(gx == edge)
+                def _():
+                    start, size = PARTS[part]
+                    self.bufs[slot][pl.ds(start, size), pl.ds(HY, TY)] = jnp.zeros((size, TY), jnp.bfloat16)
+
+                self.columns(slot, part)
+
+        def complete(self, slot):
+            for part in PARTS:
+                for side in (0, 1):
+                    self.copies["y", slot, part, side].wait_recv()
+            for side, edge in ((0, 0), (HY + TY, GRID_Y - 1)):
+                @pl.when(gy == edge)
+                def _():
+                    self.bufs[slot][:, pl.ds(side, HY)] = jnp.zeros((RX, HY), jnp.bfloat16)
+
+        def finish(self):
+            for copy in self.copies.values():
+                copy.wait_send()
+
+    first = Exchange(e_refs, 0)
+    first.along_views()
 
     parameter_copies = []
     for step in range(1, VIEWS):
@@ -97,147 +198,59 @@
             copy.start()
             parameter_copies.append(copy)
 
-    class Exchange:
-        def __init__(self, bufs, which):
-            self.bufs, self.which, self.copies = bufs, which, {}
-
-        def send(self, key, sem, src, dst, device):
-            copy = pltpu.make_async_remote_copy(
-                src_ref=src, dst_ref=dst,
-                send_sem=send_sems.at[self.which, sem], recv_sem=recv_sems.at[self.which, sem],
-                device_id=device, device_id_type=MESH,
-            )
+    def tables(first_slot, count):
+        local = [
+            pltpu.make_async_copy(src.at[pl.ds(first_slot, count)], dst.at[pl.ds(first_slot, count)], p_local.at[k])
+            for k, (src, dst) in enumerate(((sh_v, sh_s), (tp_v, tp_s)))
+        ]
+        for copy in local:
             copy.start()
-            self.copies[key] = copy
-
-        def region(self, slot, rows, cols):
-            return self.bufs[slot].at[pl.ds(*rows), pl.ds(*cols)]
-
-        def along_view(self, src_slot, dst_slot, part, sem, step):
-            rows = PARTS[part]
-            self.send(
-                ("x", dst_slot, part), sem,
-                self.region(src_slot, rows, (HY, TY)), self.region(dst_slot, rows, (HY, TY)),
-                to_view(step),
-            )
-
-        def begin(self):
-            self.along_view(0, 3, "a", 0, 1)
-            self.along_view(0, 1, "b", 1, -1)
-            self.along_view(0, 3, "b", 2, 1)
-            self.along_view(0, 1, "a", 3, -1)
-            self.spread(0, "a")
-            self.spread(0, "b")
-
-        def columns(self, slot, part):
-            rows = PARTS[part]
-            sem = Y_BASE + 8 * slot + 2 * PART_ID[part]
-            self.send(
-                ("y", slot, part, 0), sem,
-                self.region(slot, rows, (HY, HY)), self.region(slot, rows, (HY + TY, HY)), to_col(-1),
-            )
-            self.send(
-                ("y", slot, part, 1), sem + 1,
-                self.region(slot, rows, (TY, HY)), self.region(slot, rows, (0, HY)), to_col(1),
-            )
-
-        def spread(self, slot, part):
-            if part == "a":
-                self.send(
-                    ("z", slot, "bottom"), Z_BASE + 2 * slot,
-                    self.region(slot, (HX, HX), (HY, TY)),
-                    self.region(slot, (HX + TX, HX), (HY, TY)), to_row(-1),
-                )
-            else:
-                self.send(
-                    ("z", slot, "top"), Z_BASE + 2 * slot + 1,
-                    self.region(slot, (TX, HX), (HY, TY)),
-                    self.region(slot, (0, HX), (HY, TY)), to_row(1),
-                )
-            self.columns(slot, part)
-
-        def arrive(self, slot, part):
-            self.copies["x", slot, part].wait_recv()
-            if slot == 3 and part == "a":
-                self.along_view(3, 2, "a", 4, 1)
-            if slot == 1 and part == "b":
-                self.along_view(1, 2, "b", 5, -1)
-            self.spread(slot, part)
-
-        def corners(self, slot):
-            for part, edge in (("top", 0), ("bottom", grid_x - 1)):
-                self.copies["z", slot, part].wait_recv()
-
-                @pl.when(gx == edge)
-                def _():
-                    start, size = PARTS[part]
-                    self.bufs[slot][pl.ds(start, size), pl.ds(HY, TY)] = jnp.zeros((size, TY), jnp.bfloat16)
-
-                self.columns(slot, part)
-
-        def complete(self, slot):
-            for part in PARTS:
-                for side in (0, 1):
-                    self.copies["y", slot, part, side].wait_recv()
-            for side, edge in ((0, 0), (HY + TY, GRID_Y - 1)):
-                @pl.when(gy == edge)
-                def _():
-                    self.bufs[slot][:, pl.ds(side, HY)] = jnp.zeros((RX, HY), jnp.bfloat16)
-
-        def finish(self):
-            for copy in self.copies.values():
-                copy.wait_send()
-
-    first = Exchange(e_refs, 0)
-    first.begin()
-
-    def clear(pair, carry):
-        y_ref[pair, 0:32, 0:128] = jnp.zeros((32, 128), jnp.bfloat16)
-        y_ref[pair, 352:512, 0:128] = jnp.zeros((160, 128), jnp.bfloat16)
-        y_ref[pair, 0:160, 128:256] = jnp.zeros((160, 128), jnp.bfloat16)
-        y_ref[pair, 480:512, 128:256] = jnp.zeros((32, 128), jnp.bfloat16)
-        return carry
-
-    lax.fori_loop(0, VIEWS * PLANES, clear, 0)
-
-    for copy in parameter_copies:
-        copy.wait_recv()
-    local = [pltpu.make_async_copy(sh_v, sh_s, p_local.at[0]), pltpu.make_async_copy(tp_v, tp_s, p_local.at[1])]
-    for copy in local:
-        copy.start()
-    for copy in local:
-        copy.wait()
+        for copy in local:
+            copy.wait()
+
+    first.own()
+    tables(0, 1)
 
     column_low = jnp.where(gy == 0, 0, -FAR)
     column_high = jnp.where(gy == GRID_Y - 1, TY, FAR)
     row_low = jnp.where(gx == 0, 0, -FAR)
     row_high = jnp.where(gx == grid_x - 1, TX, FAR)
 
+    row16 = lax.broadcasted_iota(jnp.int32, (16, 128), 0)
+    col16 = lax.broadcasted_iota(jnp.int32, (16, 128), 1)
+
+    def band(distance, first, before, middle, after):
+        return jnp.where(
+            distance == first, before,
+            jnp.where(distance == first + 1, middle, jnp.where(distance == first + 2, after, 0.0)),
+        ).astype(jnp.bfloat16)
+
     def build(slot):
         def one(z, carry):
+            pair = slot * PLANES + z
+            y_ref[pair, 0:32, 0:128] = jnp.zeros((32, 128), jnp.bfloat16)
+            y_ref[pair, 352:512, 0:128] = jnp.zeros((160, 128), jnp.bfloat16)
+            y_ref[pair, 0:160, 128:256] = jnp.zeros((160, 128), jnp.bfloat16)
+            y_ref[pair, 480:512, 128:256] = jnp.zeros((32, 128), jnp.bfloat16)
             shear = sh_s[0, 1, z]
-            d = sh_s[slot, 1, z] - shear
+            first = sh_s[slot, 1, z] - shear - 1 + (HY - 32)
             a0, a1 = tp_s[0, 2, z], tp_s[0, 3, z]
             b0, b1 = tp_s[slot, 2, z], tp_s[slot, 3, z]
-            col = lax.broadcasted_iota(jnp.int32, (1, 128), 1)
-            distance = (
-                lax.broadcasted_iota(jnp.int32, (320, 128), 0)
-                - lax.broadcasted_iota(jnp.int32, (320, 128), 1)
-                + (32 - HY)
-            )
-            hit = [distance == d + k for k in (-1, 0, 1)]
             low, high = shear + column_low, shear + column_high
-            for tile_start, in0, in1 in (
-                (0, col >= low, col >= low - 1),
-                (128, col + 128 < high, col + 128 < high - 1),
+            weights = []
+            for in0, in1 in (
+                (col16 >= low, col16 >= low - 1),
+                (col16 + 128 < high, col16 + 128 < high - 1),
             ):
-                before = jnp.where(in0, a0 * b1, 0.0)
-                middle = jnp.where(in0, a0 * b0, 0.0) + jnp.where(in1, a1 * b1, 0.0)
-                after = jnp.where(in1, a1 * b0, 0.0)
-                value = jnp.where(hit[0], before, jnp.where(hit[1], middle, jnp.where(hit[2], after, 0.0)))
-                y_ref[slot * PLANES + z, pl.ds(32 + tile_start, 320), pl.ds(tile_start, 128)] = value.astype(
-                    jnp.bfloat16
-                )
+                weights.append((
+                    jnp.where(in0, a0 * b1, 0.0),
+                    jnp.where(in0, a0 * b0, 0.0) + jnp.where(in1, a1 * b1, 0.0),
+                    jnp.where(in1, a1 * b0, 0.0),
+                ))
+            for r in range(0, 320, 16):
+                distance = row16 - col16 + r
+                y_ref[pair, pl.ds(32 + r, 16), 0:128] = band(distance, first, *weights[0])
+                y_ref[pair, pl.ds(160 + r, 16), 128:256] = band(distance, first, *weights[1])
             return carry
 
         lax.fori_loop(0, PLANES, one, 0)
@@ -255,18 +268,20 @@
                 scalars.append((m, a0 * b1, a0 * b0, a1 * b1, a1 * b0, shear + row_low, shear + row_high))
             for u, block, row_start, size in BAND:
                 m, am, az, bz, bp, low, high = scalars[u]
-                row = lax.broadcasted_iota(jnp.int32, (size, 128), 0) + row_start
-                distance = lax.broadcasted_iota(jnp.int32, (size, 128), 1) - row + 128 * block
-                hit = [distance == m + k for k in (0, 1, 2)]
-                for half, in0, in1 in (
-                    (0, row >= low, row >= low - 1),
-                    (1, row + 128 < high, row + 128 < high - 1),
-                ):
-                    before = jnp.where(in0, am, 0.0)
-                    middle = jnp.where(in0, az, 0.0) + jnp.where(in1, bz, 0.0)
-                    after = jnp.where(in1, bp, 0.0)
-                    value = jnp.where(hit[0], before, jnp.where(hit[1], middle, jnp.where(hit[2], after, 0.0)))
-                    x_ref[slot, half, g, pl.ds(row_start, size), pl.ds(128 * block, 128)] = value.astype(jnp.bfloat16)
+                plain = (am, az + bz, bp)
+                for r in range(row_start, row_start + size, 16):
+                    distance = col16 - row16 + (128 * block - r)
+                    for half in (0, 1):
+                        weights = plain
+                        if (half == 0 and r < 48) or (half == 1 and r >= 80):
+                            row = row16 + (r + 128 * half)
+                            in0, in1 = (row >= low, row >= low - 1) if half == 0 else (row < high, row < high - 1)
+                            weights = (
+                                jnp.where(in0, am, 0.0),
+                                jnp.where(in0, az, 0.0) + jnp.where(in1, bz, 0.0),
+                                jnp.where(in1, bp, 0.0),
+                            )
+                        x_ref[slot, half, g, pl.ds(r, 16), pl.ds(128 * block, 128)] = band(distance, m, *weights)
             return carry
 
         lax.fori_loop(0, PLANES // GROUP, one, 0)
@@ -278,14 +293,15 @@
             t = jnp.dot(
                 src_ref[pl.ds(start, WINDOW), :], y_ref[slot * PLANES + z], preferred_element_type=jnp.float32
             ).astype(jnp.bfloat16)
-            upper_ref[pl.ds(STRIP * z, STRIP), :] = t[0:STRIP]
-            lower_ref[pl.ds(STRIP * z, STRIP), :] = t[128 : 128 + STRIP]
-        for half, t_ref in enumerate((upper_ref, lower_ref)):
+            strip = pl.ds(STRIP * (z % GROUP), STRIP)
+            strip_refs[0][z // GROUP, strip, :] = t[0:STRIP]
+            strip_refs[1][z // GROUP, strip, :] = t[128 : 128 + STRIP]
+        for half, t_ref in enumerate(strip_refs[0:2]):
             total = out_ref[pl.ds(128 * half, 128), :]
             for g in range(PLANES // GROUP):
                 total = total + jnp.dot(
                     x_ref[slot, half, g],
-                    t_ref[pl.ds(GROUP * STRIP * g, GROUP * STRIP), :],
+                    t_ref[g],
                     preferred_element_type=jnp.float32,
                 )
             out_ref[pl.ds(128 * half, 128), :] = total
@@ -376,8 +392,8 @@
                 ).astype(jnp.bfloat16)
         for u in range(GROUP):
             z = GROUP * chunk + u
-            for k, (ref, first) in enumerate(((vol_ref, 0), (vol_ref, 128), (back_ref, 0), (back_ref, 128))):
-                ref[0, z, pl.ds(first, 128), :] = jnp.dot(
+            for k, (ref, first) in enumerate(((0, 0), (0, 128), (1, 0), (1, 128))):
+                back_refs[ref][z, pl.ds(first, 128), :] = jnp.dot(
                     bx_ref[u], strip_refs[k][u], preferred_element_type=jnp.float32
                 )
 
@@ -386,6 +402,9 @@
 
     build(0)
     build_rows(0)
+    for copy in parameter_copies:
+        copy.wait_recv()
+    tables(1, VIEWS - 1)
     for slot, part in ((3, "a"), (1, "b"), (3, "b"), (1, "a")):
         first.arrive(slot, part)
     first.corners(0)
@@ -406,7 +425,8 @@
 
     second = Exchange(f_refs, 1)
     f_refs[0][pl.ds(HX, TX), pl.ds(HY, TY)] = q_ref[...].astype(jnp.bfloat16)
-    second.begin()
+    second.along_views()
+    second.own()
     second.corners(0)
     for slot, part in ((3, "a"), (1, "b"), (3, "b"), (1, "a")):
         second.arrive(slot, part)
@@ -442,7 +462,7 @@
     weight1 = alpha1 * alpha0
 
     def combine(z, carry):
-        vol_ref[0, z] = weight0 * vol_ref[0, z] - weight1 * back_ref[0, z]
+        vol_ref[0, z] = (weight0 * back_refs[0][z] - weight1 * back_refs[1][z]).astype(jnp.bfloat16)
         return carry
 
     lax.fori_loop(0, PLANES, combine, 0)
@@ -456,30 +476,36 @@
     sums.finish()
 
 
+def write_kernel(vol_ref, res_ref, vol_out, res_out):
+    vol_out[...] = vol_ref[...].astype(jnp.float32)
+    res_out[...] = res_ref[...]
+
+
 def local(grid_x, measured, shears, taps):
     f32, bf16 = jnp.float32, jnp.bfloat16
     vmem = pl.BlockSpec(memory_space=pltpu.VMEM)
     partners = VIEWS + GRID_Y + grid_x
-    return pl.pallas_call(
+    hbm = pl.BlockSpec(memory_space=pltpu.HBM)
+    volume, residual = pl.pallas_call(
         functools.partial(solve_kernel, grid_x),
         name="solve",
         out_shape=(
-            jax.ShapeDtypeStruct((1, PLANES, TX, TY), f32),
+            jax.ShapeDtypeStruct((1, PLANES, TX, TY), bf16),
             jax.ShapeDtypeStruct((1, 1, TX, TY), f32),
         ),
-        in_specs=[pl.BlockSpec(memory_space=pl.ANY), vmem, vmem],
+        in_specs=[hbm, hbm, hbm],
         out_specs=(vmem, vmem),
         scratch_shapes=[
             pltpu.VMEM((TX, TY), f32),
+            pltpu.VMEM((2, PLANES), jnp.int32),
+            pltpu.VMEM((4, PLANES), bf16),
             [pltpu.VMEM((RX, RY), bf16)] * VIEWS,
             [pltpu.VMEM((RX, RY), bf16)] * VIEWS,
             pltpu.VMEM((VIEWS * PLANES, RY, TY), bf16),
             pltpu.VMEM((VIEWS, 2, PLANES // GROUP, 128, GROUP * STRIP), bf16),
-            pltpu.VMEM((PLANES * STRIP, TY), bf16),
-            pltpu.VMEM((PLANES * STRIP, TY), bf16),
             pltpu.VMEM((TX, TY), f32),
             pltpu.VMEM((TX, TY), f32),
-            pltpu.VMEM((1, PLANES, TX, TY), f32),
+            [pltpu.VMEM((PLANES, TX, TY), f32)] * 2,
             pltpu.VMEM((GROUP * VIEWS, RY, TY), bf16),
             pltpu.VMEM((GROUP, 128, VIEWS * STRIP), bf16),
             [pltpu.VMEM((GROUP, VIEWS * STRIP, TY), bf16)] * 4,
@@ -502,6 +528,23 @@
             collective_id=0, has_side_effects=True, vmem_limit_bytes=50 * 1024 * 1024
         ),
     )(measured, jnp.transpose(shears, (0, 2, 1)), jnp.transpose(taps, (0, 2, 1)))
+    return pl.pallas_call(
+        write_kernel,
+        name="write",
+        grid=(4,),
+        out_shape=(
+            jax.ShapeDtypeStruct((1, PLANES, TX, TY), f32),
+            jax.ShapeDtypeStruct((1, 1, TX, TY), f32),
+        ),
+        in_specs=[
+            pl.BlockSpec((1, PLANES // 4, TX, TY), lambda i: (0, i, 0, 0)),
+            pl.BlockSpec((1, 1, TX // 4, TY), lambda i: (0, 0, i, 0)),
+        ],
+        out_specs=(
+            pl.BlockSpec((1, PLANES // 4, TX, TY), lambda i: (0, i, 0, 0)),
+            pl.BlockSpec((1, 1, TX // 4, TY), lambda i: (0, 0, i, 0)),
+        ),
+    )(volume, residual)
 
 
 def solution(mesh):

time: 82.4 us -> 80 us (0.971)
  local copies, waits for them, and re-layouts: 7.6 us -> 4.34 us
    pallas_call x0 -> x1, Pallas kernels: none -> 4.23 us  [local(): pl.pallas_call(write_kernel, name='write', grid=(4,), out_shape=(jax.Shap...]
    pallas_call x1, Pallas kernels: 73.9 us -> 70.5 us  [local(): pl.pallas_call(functools.partial(solve_kernel, grid_x), name='solve', out...]
    unnamed x8 -> x10, local copies, waits for them, and re-layouts: 7.6 us -> 4.34 us
where the time goes in v4:
time: 80 us; the launch traced here: 79.7 us
  Pallas kernels  74.7 us (93%)
  local copies, waits for them, and re-layouts  4.34 us (5%)
    pallas_call x1, Pallas kernels, local(): pl.pallas_call(functools.partial(solve_kernel, grid_x), name='solve', out...  70.5 us
    unnamed x10, local copies, waits for them, and re-layouts  4.34 us
    pallas_call x1, Pallas kernels, local(): pl.pallas_call(write_kernel, name='write', grid=(4,), out_shape=(jax.Shap...  4.23 us

profile of v4, /device:TPU:1, one launch (start us, length us, event | category | flops | bytes accessed | tf_op | source)
XLA Modules:
  0.0 79.7 jit_solution(17150299503518936122)
XLA Ops:
  0.6 0.0 copy-start.2
  0.6 0.9 %copy-done.2 = f32[1,1,256,256]{3,2,1,0:T(8,128)S(1)} copy-done((f32[1,1,256,256]{3,2,1,0:T(8,128)S(1)}, f32[1,1,256,256]{3,2,1,0:T(8,128)}, u32[]{:S(2)}) %copy-start.2) | copy-done | bytes 262168
  1.6 0.0 copy-start.3
  1.6 0.7 copy-done.3
  2.3 0.0 copy-start.4
  2.3 0.7 copy-done.4
  2.9 70.5 %solve.1 = (bf16[1,16,256,256]{3,2,1,0:T(8,128)(2,1)S(1)}, f32[1,1,256,256]{3,2,1,0:T(8,128)S(1)}) custom-call(f32[1,1,256,256]{3,2,1,0:T(8,128)S(1)} %copy-done.2, s32[1,2,16]{2,1,0:T(2,128)S(1)} %bitcast.2, bf16[1,4,16]{2,1,0:T(4,128)(2,1)S(1)} %bitcast.3), custom_call_target="tpu_custom_call" | custom-call | tf_op jit(solution)/shard_map/solve/pallas_call | solution.py:489
  73.4 0.0 copy-start
  73.5 1.3 %copy-done = bf16[1,16,256,256]{3,2,1,0:T(8,128)(2,1)} copy-done((bf16[1,16,256,256]{3,2,1,0:T(8,128)(2,1)}, bf16[1,16,256,256]{3,2,1,0:T(8,128)(2,1)S(1)}, u32[]{:S(2)}) %copy-start) | copy-done | bytes 2097176
  74.8 0.0 copy-start.1
  74.8 0.7 copy-done.1
  75.5 4.2 %write.1 = (f32[1,16,256,256]{3,2,1,0:T(8,128)}, f32[1,1,256,256]{3,2,1,0:T(8,128)}) custom-call(bf16[1,16,256,256]{3,2,1,0:T(8,128)(2,1)} %copy-done, f32[1,1,256,256]{3,2,1,0:T(8,128)} %copy-done.1), custom_call_target="tpu_custom_call" | custom-call | tf_op jit(solution)/shard_map/write/pallas_call | solution.py:531
Async XLA Ops:
  0.6 1.0 %copy-start.2 = (f32[1,1,256,256]{3,2,1,0:T(8,128)S(1)}, f32[1,1,256,256]{3,2,1,0:T(8,128)}, u32[]{:S(2)}) copy-start(f32[1,1,256,256]{3,2,1,0:T(8,128)} %meas_hbm.1) | copy-start | bytes 786436
  1.6 0.7 copy-start.3
  2.3 0.7 copy-start.4
  73.4 1.3 %copy-start = (bf16[1,16,256,256]{3,2,1,0:T(8,128)(2,1)}, bf16[1,16,256,256]{3,2,1,0:T(8,128)(2,1)S(1)}, u32[]{:S(2)}) copy-start(bf16[1,16,256,256]{3,2,1,0:T(8,128)(2,1)S(1)} %get-tuple-element.4.vol_ref) | copy-start | bytes 6291460
  74.8 0.7 copy-start.1

commit v5 on v4

--- a/solution.py
+++ b/solution.py
@@ -18,6 +18,7 @@
 RY = TY + 2 * HY
 WINDOW = 288
 STRIP = 160
+WRITE_PLANES = 2
 GROUP = 4
 BAND = (
     (0, 0, 0, 128), (0, 1, 96, 32), (1, 1, 0, 96), (1, 2, 64, 64),
@@ -184,7 +185,6 @@
                 copy.wait_send()
 
     first = Exchange(e_refs, 0)
-    first.along_views()
 
     parameter_copies = []
     for step in range(1, VIEWS):
@@ -198,6 +198,8 @@
             copy.start()
             parameter_copies.append(copy)
 
+    first.along_views()
+
     def tables(first_slot, count):
         local = [
             pltpu.make_async_copy(src.at[pl.ds(first_slot, count)], dst.at[pl.ds(first_slot, count)], p_local.at[k])
@@ -218,12 +220,20 @@
 
     row16 = lax.broadcasted_iota(jnp.int32, (16, 128), 0)
     col16 = lax.broadcasted_iota(jnp.int32, (16, 128), 1)
-
-    def band(distance, first, before, middle, after):
-        return jnp.where(
-            distance == first, before,
-            jnp.where(distance == first + 1, middle, jnp.where(distance == first + 2, after, 0.0)),
-        ).astype(jnp.bfloat16)
+    below = (row16 - col16).astype(jnp.int16)
+    beyond = (col16 - row16).astype(jnp.int16)
+
+    def spread16(x):
+        return jnp.full((16, 128), x, jnp.int32).astype(jnp.int16)
+
+    def narrow(weights):
+        return [jnp.broadcast_to(w, (16, 128)).astype(jnp.bfloat16) for w in weights]
+
+    def band(distance, first, weights):
+        value = jnp.zeros((16, 128), jnp.bfloat16)
+        for at, weight in zip(first, weights):
+            value = jnp.where(distance == at, weight, value)
+        return value
 
     def build(slot):
         def one(z, carry):
@@ -233,7 +243,7 @@
             y_ref[pair, 0:160, 128:256] = jnp.zeros((160, 128), jnp.bfloat16)
             y_ref[pair, 480:512, 128:256] = jnp.zeros((32, 128), jnp.bfloat16)
             shear = sh_s[0, 1, z]
-            first = sh_s[slot, 1, z] - shear - 1 + (HY - 32)
+            first = [spread16(sh_s[slot, 1, z] - shear + (HY - 32 + k)) for k in (-1, 0, 1)]
             a0, a1 = tp_s[0, 2, z], tp_s[0, 3, z]
             b0, b1 = tp_s[slot, 2, z], tp_s[slot, 3, z]
             low, high = shear + column_low, shear + column_high
@@ -242,15 +252,15 @@
                 (col16 >= low, col16 >= low - 1),
                 (col16 + 128 < high, col16 + 128 < high - 1),
             ):
-                weights.append((
+                weights.append(narrow((
                     jnp.where(in0, a0 * b1, 0.0),
                     jnp.where(in0, a0 * b0, 0.0) + jnp.where(in1, a1 * b1, 0.0),
                     jnp.where(in1, a1 * b0, 0.0),
-                ))
+                )))
             for r in range(0, 320, 16):
-                distance = row16 - col16 + r
-                y_ref[pair, pl.ds(32 + r, 16), 0:128] = band(distance, first, *weights[0])
-                y_ref[pair, pl.ds(160 + r, 16), 128:256] = band(distance, first, *weights[1])
+                distance = below + jnp.int16(r)
+                y_ref[pair, pl.ds(32 + r, 16), 0:128] = band(distance, first, weights[0])
+                y_ref[pair, pl.ds(160 + r, 16), 128:256] = band(distance, first, weights[1])
             return carry
 
         lax.fori_loop(0, PLANES, one, 0)
@@ -268,20 +278,21 @@
                 scalars.append((m, a0 * b1, a0 * b0, a1 * b1, a1 * b0, shear + row_low, shear + row_high))
             for u, block, row_start, size in BAND:
                 m, am, az, bz, bp, low, high = scalars[u]
-                plain = (am, az + bz, bp)
+                plain = narrow((am, az + bz, bp))
+                first = [spread16(m + k) for k in (0, 1, 2)]
                 for r in range(row_start, row_start + size, 16):
-                    distance = col16 - row16 + (128 * block - r)
+                    distance = beyond + jnp.int16(128 * block - r)
                     for half in (0, 1):
                         weights = plain
                         if (half == 0 and r < 48) or (half == 1 and r >= 80):
                             row = row16 + (r + 128 * half)
                             in0, in1 = (row >= low, row >= low - 1) if half == 0 else (row < high, row < high - 1)
-                            weights = (
+                            weights = narrow((
                                 jnp.where(in0, am, 0.0),
                                 jnp.where(in0, az, 0.0) + jnp.where(in1, bz, 0.0),
                                 jnp.where(in1, bp, 0.0),
-                            )
-                        x_ref[slot, half, g, pl.ds(r, 16), pl.ds(128 * block, 128)] = band(distance, m, *weights)
+                            ))
+                        x_ref[slot, half, g, pl.ds(r, 16), pl.ds(128 * block, 128)] = band(distance, first, weights)
             return carry
 
         lax.fori_loop(0, PLANES // GROUP, one, 0)
@@ -353,47 +364,43 @@
 
     by_ref[...] = jnp.zeros(by_ref.shape, jnp.bfloat16)
 
-    def back(chunk):
+    def back(chunk, sources):
+        refs = [(e_refs, f_refs)[k] for k in sources]
         for u in range(GROUP):
             z = GROUP * chunk + u
             for slot in range(VIEWS):
                 place = lax.rem(view + slot, VIEWS)
                 d = sh_s[slot, 1, z]
-                distance = (
-                    lax.broadcasted_iota(jnp.int32, (224, 128), 0)
-                    - lax.broadcasted_iota(jnp.int32, (224, 128), 1)
-                    + (80 - HY)
-                )
-                value = jnp.where(
-                    distance == d, tp_s[slot, 2, z], jnp.where(distance == d - 1, tp_s[slot, 3, z], 0.0)
+                weights = narrow((tp_s[slot, 3, z], tp_s[slot, 2, z]))
+                at = [spread16(d + (HY - 80 + k)) for k in (-1, 0)]
+                pair = VIEWS * u + slot
+                for r in range(0, 224, 16):
+                    value = band(below + jnp.int16(r), at, weights)
+                    by_ref[pair, pl.ds(80 + r, 16), 0:128] = value
+                    by_ref[pair, pl.ds(208 + r, 16), 128:256] = value
+                start = lax.shift_right_logical(HX - 1 + sh_s[slot, 0, z], 4) * 16
+                rows = [ref[slot][pl.ds(start, WINDOW), :] for ref in refs]
+                t = jnp.dot(
+                    jnp.concatenate(rows, axis=0) if len(rows) > 1 else rows[0],
+                    by_ref[pair], preferred_element_type=jnp.float32,
                 ).astype(jnp.bfloat16)
-                pair = VIEWS * u + slot
-                by_ref[pair, 80:304, 0:128] = value
-                by_ref[pair, 208:432, 128:256] = value
-                start = lax.shift_right_logical(HX - 1 + sh_s[slot, 0, z], 4) * 16
-                both = jnp.concatenate(
-                    [e_refs[slot][pl.ds(start, WINDOW), :], f_refs[slot][pl.ds(start, WINDOW), :]], axis=0
-                )
-                t = jnp.dot(both, by_ref[pair], preferred_element_type=jnp.float32).astype(jnp.bfloat16)
-                for k, first in enumerate((0, 128, WINDOW, WINDOW + 128)):
+                for k in range(2 * len(refs)):
+                    first = WINDOW * (k // 2) + 128 * (k % 2)
                     strip_refs[k][u, pl.ds(STRIP * place, STRIP), :] = t[first : first + STRIP]
             for v, block, row_start, size in BAND:
                 slot = lax.rem(v - view + VIEWS, VIEWS)
                 first_row = HX - 1 + sh_s[slot, 0, z]
                 m = first_row - lax.shift_right_logical(first_row, 4) * 16 + STRIP * v
-                b0, b1 = tp_s[slot, 0, z] * (PLANES**-0.5), tp_s[slot, 1, z] * (PLANES**-0.5)
-                distance = (
-                    lax.broadcasted_iota(jnp.int32, (size, 128), 1)
-                    - lax.broadcasted_iota(jnp.int32, (size, 128), 0)
-                    + (128 * block - row_start)
-                )
-                bx_ref[u, pl.ds(row_start, size), pl.ds(128 * block, 128)] = jnp.where(
-                    distance == m, b1, jnp.where(distance == m + 1, b0, 0.0)
-                ).astype(jnp.bfloat16)
+                weights = narrow((tp_s[slot, 1, z] * (PLANES**-0.5), tp_s[slot, 0, z] * (PLANES**-0.5)))
+                at = [spread16(m + k) for k in (0, 1)]
+                for r in range(row_start, row_start + size, 16):
+                    bx_ref[u, pl.ds(r, 16), pl.ds(128 * block, 128)] = band(
+                        beyond + jnp.int16(128 * block - r), at, weights
+                    )
         for u in range(GROUP):
             z = GROUP * chunk + u
-            for k, (ref, first) in enumerate(((0, 0), (0, 128), (1, 0), (1, 128))):
-                back_refs[ref][z, pl.ds(first, 128), :] = jnp.dot(
+            for k in range(2 * len(refs)):
+                back_refs[sources[k // 2]][z, pl.ds(128 * (k % 2), 128), :] = jnp.dot(
                     bx_ref[u], strip_refs[k][u], preferred_element_type=jnp.float32
                 )
 
@@ -405,11 +412,15 @@
     for copy in parameter_copies:
         copy.wait_recv()
     tables(1, VIEWS - 1)
-    for slot, part in ((3, "a"), (1, "b"), (3, "b"), (1, "a")):
-        first.arrive(slot, part)
     first.corners(0)
+    first.arrive(3, "a")
+    first.arrive(1, "b")
     build(3)
     build_rows(3)
+    first.arrive(3, "b")
+    first.arrive(1, "a")
+    first.complete(0)
+    apply(e_refs[0], q_ref, 0)
     first.arrive(2, "a")
     first.arrive(2, "b")
     first.corners(3)
@@ -419,7 +430,7 @@
     first.corners(2)
     build(2)
     build_rows(2)
-    for slot in (0, 3, 1, 2):
+    for slot in (3, 1, 2):
         first.complete(slot)
         apply(e_refs[slot], q_ref, slot)
 
@@ -427,6 +438,7 @@
     f_refs[0][pl.ds(HX, TX), pl.ds(HY, TY)] = q_ref[...].astype(jnp.bfloat16)
     second.along_views()
     second.own()
+    back(0, (0,))
     second.corners(0)
     for slot, part in ((3, "a"), (1, "b"), (3, "b"), (1, "a")):
         second.arrive(slot, part)
@@ -436,6 +448,7 @@
     second.arrive(2, "b")
     second.corners(3)
     second.corners(1)
+    back(1, (0,))
     second.corners(2)
     for slot in (3, 1, 2):
         second.complete(slot)
@@ -444,11 +457,16 @@
     r0 = e_refs[0][pl.ds(HX, TX), pl.ds(HY, TY)].astype(jnp.float32)
     q0, p = q_ref[...], p_ref[...]
     sums = Sum([lanes(r0 * q0), lanes(q0 * q0), lanes(r0 * p), lanes(q0 * p), lanes(p * p)])
-    for stage in range(3):
-        sums.send(stage)
-        back(stage)
-        sums.receive(stage)
-    back(3)
+    sums.send(0)
+    back(2, (0, 1))
+    sums.receive(0)
+    sums.send(1)
+    back(3, (0, 1))
+    sums.receive(1)
+    sums.send(2)
+    back(0, (1,))
+    back(1, (1,))
+    sums.receive(2)
     r0q0, q0q0, r0p, q0p, pp = [sums.row(i) for i in range(5)]
     gamma0 = r0q0
     alpha0 = gamma0 / (q0q0 + TINY)
@@ -477,8 +495,13 @@
 
 
 def write_kernel(vol_ref, res_ref, vol_out, res_out):
-    vol_out[...] = vol_ref[...].astype(jnp.float32)
-    res_out[...] = res_ref[...]
+    step = pl.program_id(0)
+    planes = pl.ds(step * WRITE_PLANES, WRITE_PLANES)
+    vol_out[0] = vol_ref[0, planes].astype(jnp.float32)
+
+    @pl.when(step == 0)
+    def _():
+        res_out[...] = res_ref[...]
 
 
 def local(grid_x, measured, shears, taps):
@@ -531,18 +554,15 @@
     return pl.pallas_call(
         write_kernel,
         name="write",
-        grid=(4,),
+        grid=(PLANES // WRITE_PLANES,),
         out_shape=(
             jax.ShapeDtypeStruct((1, PLANES, TX, TY), f32),
             jax.ShapeDtypeStruct((1, 1, TX, TY), f32),
         ),
-        in_specs=[
-            pl.BlockSpec((1, PLANES // 4, TX, TY), lambda i: (0, i, 0, 0)),
-            pl.BlockSpec((1, 1, TX // 4, TY), lambda i: (0, 0, i, 0)),
-        ],
+        in_specs=[vmem, vmem],
         out_specs=(
-            pl.BlockSpec((1, PLANES // 4, TX, TY), lambda i: (0, i, 0, 0)),
-            pl.BlockSpec((1, 1, TX // 4, TY), lambda i: (0, 0, i, 0)),
+            pl.BlockSpec((1, WRITE_PLANES, TX, TY), lambda i: (0, i, 0, 0)),
+            pl.BlockSpec((1, 1, TX, TY), lambda i: (0, 0, 0, 0)),
         ),
     )(volume, residual)
 

time: 80 us -> 72.9 us (0.911)
  Pallas kernels: 74.7 us -> 67.7 us
    pallas_call x1, Pallas kernels: 70.5 us -> 62.6 us  [local(): pl.pallas_call(functools.partial(solve_kernel, grid_x), name='solve', out...]
    pallas_call x1, Pallas kernels: 4.23 us -> 5.17 us  [local(): pl.pallas_call(write_kernel, name='write', grid=(PLANES // WRITE_PLANES,)...]
where the time goes in v5:
time: 72.9 us; the launch traced here: 72.7 us
  Pallas kernels  67.7 us (93%)
  local copies, waits for them, and re-layouts  4.34 us (6%)
    pallas_call x1, Pallas kernels, local(): pl.pallas_call(functools.partial(solve_kernel, grid_x), name='solve', out...  62.6 us
    pallas_call x1, Pallas kernels, local(): pl.pallas_call(write_kernel, name='write', grid=(PLANES // WRITE_PLANES,)...  5.17 us
    unnamed x10, local copies, waits for them, and re-layouts  4.34 us

profile of v5, /device:TPU:1, one launch (start us, length us, event | category | flops | bytes accessed | tf_op | source)
XLA Modules:
  0.0 72.7 jit_solution(7246848428817885742)
XLA Ops:
  0.6 0.0 copy-start.2
  0.6 0.9 %copy-done.2 = f32[1,1,256,256]{3,2,1,0:T(8,128)S(1)} copy-done((f32[1,1,256,256]{3,2,1,0:T(8,128)S(1)}, f32[1,1,256,256]{3,2,1,0:T(8,128)}, u32[]{:S(2)}) %copy-start.2) | copy-done | bytes 262168
  1.6 0.0 copy-start.3
  1.6 0.7 copy-done.3
  2.3 0.0 copy-start.4
  2.3 0.7 copy-done.4
  2.9 62.6 %solve.1 = (bf16[1,16,256,256]{3,2,1,0:T(8,128)(2,1)S(1)}, f32[1,1,256,256]{3,2,1,0:T(8,128)S(1)}) custom-call(f32[1,1,256,256]{3,2,1,0:T(8,128)S(1)} %copy-done.2, s32[1,2,16]{2,1,0:T(2,128)S(1)} %bitcast.2, bf16[1,4,16]{2,1,0:T(4,128)(2,1)S(1)} %bitcast.3), custom_call_target="tpu_custom_call" | custom-call | tf_op jit(solution)/shard_map/solve/pallas_call | solution.py:512
  65.5 0.0 copy-start
  65.5 1.3 %copy-done = bf16[1,16,256,256]{3,2,1,0:T(8,128)(2,1)} copy-done((bf16[1,16,256,256]{3,2,1,0:T(8,128)(2,1)}, bf16[1,16,256,256]{3,2,1,0:T(8,128)(2,1)S(1)}, u32[]{:S(2)}) %copy-start) | copy-done | bytes 2097176
  66.9 0.0 copy-start.1
  66.9 0.7 copy-done.1
  67.6 5.2 %write.1 = (f32[1,16,256,256]{3,2,1,0:T(8,128)}, f32[1,1,256,256]{3,2,1,0:T(8,128)}) custom-call(bf16[1,16,256,256]{3,2,1,0:T(8,128)(2,1)} %copy-done, f32[1,1,256,256]{3,2,1,0:T(8,128)} %copy-done.1), custom_call_target="tpu_custom_call" | custom-call | tf_op jit(solution)/shard_map/write/pallas_call | solution.py:554
Async XLA Ops:
  0.6 1.0 %copy-start.2 = (f32[1,1,256,256]{3,2,1,0:T(8,128)S(1)}, f32[1,1,256,256]{3,2,1,0:T(8,128)}, u32[]{:S(2)}) copy-start(f32[1,1,256,256]{3,2,1,0:T(8,128)} %meas_hbm.1) | copy-start | bytes 786436
  1.6 0.7 copy-start.3
  2.3 0.7 copy-start.4
  65.5 1.3 %copy-start = (bf16[1,16,256,256]{3,2,1,0:T(8,128)(2,1)}, bf16[1,16,256,256]{3,2,1,0:T(8,128)(2,1)S(1)}, u32[]{:S(2)}) copy-start(bf16[1,16,256,256]{3,2,1,0:T(8,128)(2,1)S(1)} %get-tuple-element.4.vol_ref) | copy-start | bytes 6291460
  66.9 0.7 copy-start.1

commit v6 on v5

--- a/solution.py
+++ b/solution.py
@@ -28,13 +28,16 @@
 TINY = 1e-6
 MESH = pl.DeviceIdType.MESH
 
-X_SEMS = 6
-Z_BASE = X_SEMS
+Z_BASE = 9
 Y_BASE = Z_BASE + 2 * VIEWS
-N_SEMS = Y_BASE + 8 * VIEWS
-
-PARTS = {"a": (HX, TX // 2), "b": (HX + TX // 2, TX // 2), "top": (0, HX), "bottom": (HX + TX, HX)}
-PART_ID = {"a": 0, "b": 1, "top": 2, "bottom": 3}
+D_BASE = Y_BASE + 10 * VIEWS
+N_SEMS = D_BASE + 4
+
+PARTS = {
+    "first": (HX, HX), "last": (TX, HX), "middle": (2 * HX, TX - 2 * HX),
+    "top": (0, HX), "bottom": (HX + TX, HX),
+}
+PART_ID = {"first": 0, "last": 1, "middle": 2, "top": 3, "bottom": 4}
 
 
 def ring(index, step, size):
@@ -66,10 +69,14 @@
     def to_col(step):
         return at(gx, ring(gy, step, GRID_Y), view)
 
+    def to_corner(row_step, col_step):
+        return at(ring(gx, row_step, grid_x), ring(gy, col_step, GRID_Y), view)
+
     partners = (
         [to_view(s) for s in range(1, VIEWS)]
         + [to_row(s) for s in range(1, grid_x)]
         + [to_col(s) for s in range(1, GRID_Y)]
+        + [to_corner(r, c) for r in (-1, 1) for c in (-1, 1)]
     )
     barrier = pltpu.get_barrier_semaphore()
     for partner in partners:
@@ -116,18 +123,20 @@
             )
 
         def along_views(self):
-            self.along_view(0, 3, "a", 0, 1)
-            self.along_view(0, 1, "b", 1, -1)
-            self.along_view(0, 3, "b", 2, 1)
-            self.along_view(0, 1, "a", 3, -1)
+            self.along_view(0, 3, "first", 0, 1)
+            self.along_view(0, 1, "last", 1, -1)
+            self.along_view(0, 3, "last", 2, 1)
+            self.along_view(0, 1, "first", 3, -1)
+            self.along_view(0, 3, "middle", 4, 1)
+            self.along_view(0, 1, "middle", 5, -1)
 
         def own(self):
-            self.spread(0, "a")
-            self.spread(0, "b")
+            for part in ("first", "last", "middle"):
+                self.spread(0, part)
 
         def columns(self, slot, part):
             rows = PARTS[part]
-            sem = Y_BASE + 8 * slot + 2 * PART_ID[part]
+            sem = Y_BASE + 10 * slot + 2 * PART_ID[part]
             self.send(
                 ("y", slot, part, 0), sem,
                 self.region(slot, rows, (HY, HY)), self.region(slot, rows, (HY + TY, HY)), to_col(-1),
@@ -138,26 +147,30 @@
             )
 
         def spread(self, slot, part):
-            if part == "a":
-                self.send(
-                    ("z", slot, "bottom"), Z_BASE + 2 * slot,
-                    self.region(slot, (HX, HX), (HY, TY)),
-                    self.region(slot, (HX + TX, HX), (HY, TY)), to_row(-1),
-                )
-            else:
-                self.send(
-                    ("z", slot, "top"), Z_BASE + 2 * slot + 1,
-                    self.region(slot, (TX, HX), (HY, TY)),
-                    self.region(slot, (0, HX), (HY, TY)), to_row(1),
-                )
+            for k, (rim, halo, step) in enumerate((("first", "bottom", -1), ("last", "top", 1))):
+                if part == rim:
+                    self.send(
+                        ("z", slot, halo), Z_BASE + 2 * slot + k,
+                        self.region(slot, PARTS[rim], (HY, TY)),
+                        self.region(slot, PARTS[halo], (HY, TY)), to_row(step),
+                    )
+                    if slot == 2:
+                        for side, (src, dst, turn) in enumerate(((HY, HY + TY, -1), (TY, 0, 1))):
+                            self.send(
+                                ("d", halo, side), D_BASE + 2 * k + side,
+                                self.region(slot, PARTS[rim], (src, HY)),
+                                self.region(slot, PARTS[halo], (dst, HY)), to_corner(step, turn),
+                            )
             self.columns(slot, part)
 
         def arrive(self, slot, part):
             self.copies["x", slot, part].wait_recv()
-            if slot == 3 and part == "a":
-                self.along_view(3, 2, "a", 4, 1)
-            if slot == 1 and part == "b":
-                self.along_view(1, 2, "b", 5, -1)
+            if slot == 3 and part == "first":
+                self.along_view(3, 2, part, 6, 1)
+            if slot == 1 and part == "last":
+                self.along_view(1, 2, part, 7, -1)
+            if slot == 3 and part == "middle":
+                self.along_view(3, 2, part, 8, 1)
             self.spread(slot, part)
 
         def corners(self, slot):
@@ -172,9 +185,20 @@
                 self.columns(slot, part)
 
         def complete(self, slot):
+            if slot == 2:
+                for halo in ("top", "bottom"):
+                    self.copies["z", slot, halo].wait_recv()
+                    for side in (0, 1):
+                        self.copies["d", halo, side].wait_recv()
+                for halo, edge in (("top", 0), ("bottom", grid_x - 1)):
+                    @pl.when(gx == edge)
+                    def _():
+                        start, size = PARTS[halo]
+                        self.bufs[slot][pl.ds(start, size), :] = jnp.zeros((size, RY), jnp.bfloat16)
             for part in PARTS:
                 for side in (0, 1):
-                    self.copies["y", slot, part, side].wait_recv()
+                    if ("y", slot, part, side) in self.copies:
+                        self.copies["y", slot, part, side].wait_recv()
             for side, edge in ((0, 0), (HY + TY, GRID_Y - 1)):
                 @pl.when(gy == edge)
                 def _():
@@ -413,21 +437,23 @@
         copy.wait_recv()
     tables(1, VIEWS - 1)
     first.corners(0)
-    first.arrive(3, "a")
-    first.arrive(1, "b")
+    first.arrive(3, "first")
+    first.arrive(1, "last")
     build(3)
     build_rows(3)
-    first.arrive(3, "b")
-    first.arrive(1, "a")
+    first.arrive(3, "last")
+    first.arrive(1, "first")
+    first.arrive(3, "middle")
+    first.arrive(1, "middle")
     first.complete(0)
     apply(e_refs[0], q_ref, 0)
-    first.arrive(2, "a")
-    first.arrive(2, "b")
+    first.arrive(2, "first")
+    first.arrive(2, "last")
+    first.arrive(2, "middle")
     first.corners(3)
     first.corners(1)
     build(1)
     build_rows(1)
-    first.corners(2)
     build(2)
     build_rows(2)
     for slot in (3, 1, 2):
@@ -440,16 +466,17 @@
     second.own()
     back(0, (0,))
     second.corners(0)
-    for slot, part in ((3, "a"), (1, "b"), (3, "b"), (1, "a")):
-        second.arrive(slot, part)
+    for part in ("first", "last", "middle"):
+        second.arrive(3, part)
+        second.arrive(1, {"first": "last", "last": "first", "middle": "middle"}[part])
     second.complete(0)
     apply(f_refs[0], p_ref, 0)
-    second.arrive(2, "a")
-    second.arrive(2, "b")
+    second.arrive(2, "first")
+    second.arrive(2, "last")
     second.corners(3)
     second.corners(1)
+    second.arrive(2, "middle")
     back(1, (0,))
-    second.corners(2)
     for slot in (3, 1, 2):
         second.complete(slot)
         apply(f_refs[slot], p_ref, slot)
@@ -564,6 +591,7 @@
             pl.BlockSpec((1, WRITE_PLANES, TX, TY), lambda i: (0, i, 0, 0)),
             pl.BlockSpec((1, 1, TX, TY), lambda i: (0, 0, 0, 0)),
         ),
+        compiler_params=pltpu.CompilerParams(vmem_limit_bytes=16 * 1024 * 1024),
     )(volume, residual)
 
 

time: 72.9 us -> 69.8 us (0.957)
  local copies, waits for them, and re-layouts: 4.34 us -> 2.3 us
  Pallas kernels: 67.7 us -> 66.4 us
    unnamed x10 -> x6, local copies, waits for them, and re-layouts: 4.34 us -> 2.3 us
    pallas_call x1, Pallas kernels: 5.17 us -> 3.61 us  [local(): pl.pallas_call(write_kernel, name='write', grid=(PLANES // WRITE_PLANES,)...]
where the time goes in v6:
time: 69.8 us; the launch traced here: 69.3 us
  Pallas kernels  66.4 us (95%)
  local copies, waits for them, and re-layouts  2.3 us (3%)
    pallas_call x1, Pallas kernels, local(): pl.pallas_call(functools.partial(solve_kernel, grid_x), name='solve', out...  62.8 us
    pallas_call x1, Pallas kernels, local(): pl.pallas_call(write_kernel, name='write', grid=(PLANES // WRITE_PLANES,)...  3.61 us
    unnamed x6, local copies, waits for them, and re-layouts  2.3 us

profile of v6, /device:TPU:1, one launch (start us, length us, event | category | flops | bytes accessed | tf_op | source)
XLA Modules:
  0.0 69.3 jit_solution(16170775564758964548)
XLA Ops:
  0.6 0.0 copy-start
  0.6 0.9 %copy-done = f32[1,1,256,256]{3,2,1,0:T(8,128)S(1)} copy-done((f32[1,1,256,256]{3,2,1,0:T(8,128)S(1)}, f32[1,1,256,256]{3,2,1,0:T(8,128)}, u32[]{:S(2)}) %copy-start) | copy-done | bytes 262168
  1.6 0.0 copy-start.1
  1.6 0.7 copy-done.1
  2.3 0.0 copy-start.2
  2.3 0.7 copy-done.2
  2.9 62.8 %solve.1 = (bf16[1,16,256,256]{3,2,1,0:T(8,128)(2,1)S(1)}, f32[1,1,256,256]{3,2,1,0:T(8,128)S(1)}) custom-call(f32[1,1,256,256]{3,2,1,0:T(8,128)S(1)} %copy-done, s32[1,2,16]{2,1,0:T(2,128)S(1)} %bitcast.2, bf16[1,4,16]{2,1,0:T(4,128)(2,1)S(1)} %bitcast.3), custom_call_target="tpu_custom_call" | custom-call | tf_op jit(solution)/shard_map/solve/pallas_call | solution.py:539
  65.7 3.6 %write.1 = (f32[1,16,256,256]{3,2,1,0:T(8,128)}, f32[1,1,256,256]{3,2,1,0:T(8,128)}) custom-call(bf16[1,16,256,256]{3,2,1,0:T(8,128)(2,1)S(1)} %get-tuple-element.4.vol_ref, f32[1,1,256,256]{3,2,1,0:T(8,128)S(1)} %get-tuple-element.5.res_ref), custom_call_target="tpu_custom_call" | custom-call | tf_op jit(solution)/shard_map/write/pallas_call | solution.py:581
Async XLA Ops:
  0.6 1.0 %copy-start = (f32[1,1,256,256]{3,2,1,0:T(8,128)S(1)}, f32[1,1,256,256]{3,2,1,0:T(8,128)}, u32[]{:S(2)}) copy-start(f32[1,1,256,256]{3,2,1,0:T(8,128)} %meas_hbm.1) | copy-start | bytes 786436
  1.6 0.7 copy-start.1
  2.3 0.7 copy-start.2

commit v7 on v6

--- a/solution.py
+++ b/solution.py
@@ -18,7 +18,6 @@
 RY = TY + 2 * HY
 WINDOW = 288
 STRIP = 160
-WRITE_PLANES = 2
 GROUP = 4
 BAND = (
     (0, 0, 0, 128), (0, 1, 96, 32), (1, 1, 0, 96), (1, 2, 64, 64),
@@ -48,7 +47,7 @@
     grid_x,
     meas_hbm, sh_hbm, tp_hbm,
     vol_ref, res_ref,
-    meas_ref, sh_ref, tp_ref, e_refs, f_refs, y_ref, x_ref, q_ref, p_ref, back_refs, by_ref, bx_ref, strip_refs,
+    meas_ref, sh_ref, tp_ref, e_refs, f_refs, field_ref, y_ref, x_ref, q_ref, p_ref, back_refs, by_ref, bx_ref, strip_refs,
     sh_v, tp_v, sh_s, tp_s, ra_ref, rb_ref, rc_ref,
     send_sems, recv_sems, p_send, p_recv, p_local, a_send, a_recv,
 ):
@@ -235,7 +234,6 @@
             copy.wait()
 
     first.own()
-    tables(0, 1)
 
     column_low = jnp.where(gy == 0, 0, -FAR)
     column_high = jnp.where(gy == GRID_Y - 1, TY, FAR)
@@ -261,7 +259,7 @@
 
     def build(slot):
         def one(z, carry):
-            pair = slot * PLANES + z
+            pair = (slot - 1) * PLANES + z
             y_ref[pair, 0:32, 0:128] = jnp.zeros((32, 128), jnp.bfloat16)
             y_ref[pair, 352:512, 0:128] = jnp.zeros((160, 128), jnp.bfloat16)
             y_ref[pair, 0:160, 128:256] = jnp.zeros((160, 128), jnp.bfloat16)
@@ -316,17 +314,51 @@
                                 jnp.where(in0, az, 0.0) + jnp.where(in1, bz, 0.0),
                                 jnp.where(in1, bp, 0.0),
                             ))
-                        x_ref[slot, half, g, pl.ds(r, 16), pl.ds(128 * block, 128)] = band(distance, first, weights)
+                        x_ref[slot - 1, half, g, pl.ds(r, 16), pl.ds(128 * block, 128)] = band(distance, first, weights)
             return carry
 
         lax.fori_loop(0, PLANES // GROUP, one, 0)
+
+    def fields():
+        row = lax.broadcasted_iota(jnp.int32, (TX, 128), 0)
+
+        def factors(shear, w0, w1, low, high, scale):
+            in0 = (row >= shear + low) & (row < shear + high)
+            in1 = (row >= shear + low - 1) & (row < shear + high - 1)
+            cross = w0 * w1 * scale
+            return jnp.concatenate([
+                jnp.where(in0, cross, 0.0),
+                jnp.where(in0, w0 * w0 * scale, 0.0) + jnp.where(in1, w1 * w1 * scale, 0.0),
+                jnp.where(in1, cross, 0.0),
+            ], axis=0).astype(jnp.bfloat16)
+
+        along_x = factors(sh_v[0, 0:1, :], tp_v[0, 0:1, :], tp_v[0, 1:2, :], row_low, row_high, 1.0 / PLANES)
+        along_y = factors(sh_v[0, 1:2, :], tp_v[0, 2:3, :], tp_v[0, 3:4, :], column_low, column_high, 1.0)
+        field_ref[...] = lax.dot_general(
+            along_x, along_y, (((1,), (1,)), ((), ())), preferred_element_type=jnp.float32
+        )
+
+    def stencil(src_ref, out_ref):
+        def rows(i, carry):
+            start = i * 64
+            x = src_ref[pl.ds(pl.multiple_of(HX - 16 + start, 16), 96), :].astype(jnp.float32)
+            total = jnp.zeros((64, TY), jnp.float32)
+            for l in range(3):
+                shifted = pltpu.roll(x, (RY + 1 - l) % RY, 1)[:, HY : HY + TY]
+                for k in range(3):
+                    term = pltpu.roll(shifted, (96 + 1 - k) % 96, 0)[16:80]
+                    total = total + term * field_ref[pl.ds(pl.multiple_of(TX * k + start, 64), 64), TY * l : TY * (l + 1)]
+            out_ref[pl.ds(pl.multiple_of(start, 64), 64), :] = total
+            return carry
+
+        lax.fori_loop(0, TX // 64, rows, 0)
 
     def apply(src_ref, out_ref, slot):
         for z in range(PLANES):
             first_row = HX - 1 + sh_s[slot, 0, z] - sh_s[0, 0, z]
             start = lax.shift_right_logical(first_row, 4) * 16
             t = jnp.dot(
-                src_ref[pl.ds(start, WINDOW), :], y_ref[slot * PLANES + z], preferred_element_type=jnp.float32
+                src_ref[pl.ds(start, WINDOW), :], y_ref[(slot - 1) * PLANES + z], preferred_element_type=jnp.float32
             ).astype(jnp.bfloat16)
             strip = pl.ds(STRIP * (z % GROUP), STRIP)
             strip_refs[0][z // GROUP, strip, :] = t[0:STRIP]
@@ -335,7 +367,7 @@
             total = out_ref[pl.ds(128 * half, 128), :]
             for g in range(PLANES // GROUP):
                 total = total + jnp.dot(
-                    x_ref[slot, half, g],
+                    x_ref[slot - 1, half, g],
                     t_ref[g],
                     preferred_element_type=jnp.float32,
                 )
@@ -428,14 +460,10 @@
                     bx_ref[u], strip_refs[k][u], preferred_element_type=jnp.float32
                 )
 
-    q_ref[...] = jnp.zeros((TX, TY), jnp.float32)
-    p_ref[...] = jnp.zeros((TX, TY), jnp.float32)
-
-    build(0)
-    build_rows(0)
+    fields()
     for copy in parameter_copies:
         copy.wait_recv()
-    tables(1, VIEWS - 1)
+    tables(0, VIEWS)
     first.corners(0)
     first.arrive(3, "first")
     first.arrive(1, "last")
@@ -446,7 +474,7 @@
     first.arrive(3, "middle")
     first.arrive(1, "middle")
     first.complete(0)
-    apply(e_refs[0], q_ref, 0)
+    stencil(e_refs[0], q_ref)
     first.arrive(2, "first")
     first.arrive(2, "last")
     first.arrive(2, "middle")
@@ -470,7 +498,7 @@
         second.arrive(3, part)
         second.arrive(1, {"first": "last", "last": "first", "middle": "middle"}[part])
     second.complete(0)
-    apply(f_refs[0], p_ref, 0)
+    stencil(f_refs[0], p_ref)
     second.arrive(2, "first")
     second.arrive(2, "last")
     second.corners(3)
@@ -521,14 +549,15 @@
     sums.finish()
 
 
-def write_kernel(vol_ref, res_ref, vol_out, res_out):
-    step = pl.program_id(0)
-    planes = pl.ds(step * WRITE_PLANES, WRITE_PLANES)
-    vol_out[0] = vol_ref[0, planes].astype(jnp.float32)
-
-    @pl.when(step == 0)
-    def _():
-        res_out[...] = res_ref[...]
+def write_kernel(vol_ref, res_ref, vol_out, res_out, wide_ref, sems):
+    copies = [pltpu.make_async_copy(res_ref, res_out, sems.at[PLANES])]
+    copies[0].start()
+    for z in range(PLANES):
+        wide_ref[z] = vol_ref[0, z].astype(jnp.float32)
+        copies.append(pltpu.make_async_copy(wide_ref.at[z], vol_out.at[0, z], sems.at[z]))
+        copies[-1].start()
+    for copy in copies:
+        copy.wait()
 
 
 def local(grid_x, measured, shears, taps):
@@ -551,8 +580,9 @@
             pltpu.VMEM((4, PLANES), bf16),
             [pltpu.VMEM((RX, RY), bf16)] * VIEWS,
             [pltpu.VMEM((RX, RY), bf16)] * VIEWS,
-            pltpu.VMEM((VIEWS * PLANES, RY, TY), bf16),
-            pltpu.VMEM((VIEWS, 2, PLANES // GROUP, 128, GROUP * STRIP), bf16),
+            pltpu.VMEM((3 * TX, 3 * TY), f32),
+            pltpu.VMEM(((VIEWS - 1) * PLANES, RY, TY), bf16),
+            pltpu.VMEM((VIEWS - 1, 2, PLANES // GROUP, 128, GROUP * STRIP), bf16),
             pltpu.VMEM((TX, TY), f32),
             pltpu.VMEM((TX, TY), f32),
             [pltpu.VMEM((PLANES, TX, TY), f32)] * 2,
@@ -581,16 +611,13 @@
     return pl.pallas_call(
         write_kernel,
         name="write",
-        grid=(PLANES // WRITE_PLANES,),
         out_shape=(
             jax.ShapeDtypeStruct((1, PLANES, TX, TY), f32),
             jax.ShapeDtypeStruct((1, 1, TX, TY), f32),
         ),
         in_specs=[vmem, vmem],
-        out_specs=(
-            pl.BlockSpec((1, WRITE_PLANES, TX, TY), lambda i: (0, i, 0, 0)),
-            pl.BlockSpec((1, 1, TX, TY), lambda i: (0, 0, 0, 0)),
-        ),
+        out_specs=(hbm, hbm),
+        scratch_shapes=[pltpu.VMEM((PLANES, TX, TY), f32), pltpu.SemaphoreType.DMA((PLANES + 1,))],
         compiler_params=pltpu.CompilerParams(vmem_limit_bytes=16 * 1024 * 1024),
     )(volume, residual)
 

time: 69.8 us -> 67.8 us (0.971)
  Pallas kernels: 66.4 us -> 64.5 us
    pallas_call x1, Pallas kernels: 3.61 us -> 2.23 us  [local(): pl.pallas_call(write_kernel, name='write', out_shape=(jax.ShapeDtypeStruc...]
where the time goes in v7:
time: 67.8 us; the launch traced here: 67.6 us
  Pallas kernels  64.5 us (95%)
  local copies, waits for them, and re-layouts  2.3 us (3%)
  between operations  0.81 us (1%)
    pallas_call x1, Pallas kernels, local(): pl.pallas_call(functools.partial(solve_kernel, grid_x), name='solve', out...  62.3 us
    unnamed x6, local copies, waits for them, and re-layouts  2.3 us
    pallas_call x1, Pallas kernels, local(): pl.pallas_call(write_kernel, name='write', out_shape=(jax.ShapeDtypeStruc...  2.23 us

profile of v7, /device:TPU:1, one launch (start us, length us, event | category | flops | bytes accessed | tf_op | source)
XLA Modules:
  0.0 67.6 jit_solution(5013536364742651523)
XLA Ops:
  0.6 0.0 copy-start
  0.6 0.9 %copy-done = f32[1,1,256,256]{3,2,1,0:T(8,128)S(1)} copy-done((f32[1,1,256,256]{3,2,1,0:T(8,128)S(1)}, f32[1,1,256,256]{3,2,1,0:T(8,128)}, u32[]{:S(2)}) %copy-start) | copy-done | bytes 262168
  1.6 0.0 copy-start.1
  1.6 0.7 %copy-done.1 = s32[1,16,2]{1,2,0:T(2,128)S(1)} copy-done((s32[1,16,2]{1,2,0:T(2,128)S(1)}, s32[1,16,2]{1,2,0:T(2,128)}, u32[]{:S(2)}) %copy-start.1) | copy-done | bytes 152
  2.3 0.0 copy-start.2
  2.3 0.7 %copy-done.2 = bf16[1,16,4]{1,2,0:T(4,128)(2,1)S(1)} copy-done((bf16[1,16,4]{1,2,0:T(4,128)(2,1)S(1)}, bf16[1,16,4]{1,2,0:T(4,128)(2,1)}, u32[]{:S(2)}) %copy-start.2) | copy-done | bytes 152
  2.9 62.3 %solve.1 = (bf16[1,16,256,256]{3,2,1,0:T(8,128)(2,1)S(1)}, f32[1,1,256,256]{3,2,1,0:T(8,128)S(1)}) custom-call(f32[1,1,256,256]{3,2,1,0:T(8,128)S(1)} %copy-done, s32[1,2,16]{2,1,0:T(2,128)S(1)} %bitcast.2, bf16[1,4,16]{2,1,0:T(4,128)(2,1)S(1)} %bitcast.3), custom_call_target="tpu_custom_call" | custom-call | tf_op jit(solution)/shard_map/solve/pallas_call | solution.py:568
  65.2 2.2 %write.1 = (f32[1,16,256,256]{3,2,1,0:T(8,128)}, f32[1,1,256,256]{3,2,1,0:T(8,128)}) custom-call(bf16[1,16,256,256]{3,2,1,0:T(8,128)(2,1)S(1)} %get-tuple-element.4.vol_ref, f32[1,1,256,256]{3,2,1,0:T(8,128)S(1)} %get-tuple-element.5.res_ref), custom_call_target="tpu_custom_call" | custom-call | tf_op jit(solution)/shard_map/write/pallas_call | solution.py:611
Async XLA Ops:
  0.6 1.0 %copy-start = (f32[1,1,256,256]{3,2,1,0:T(8,128)S(1)}, f32[1,1,256,256]{3,2,1,0:T(8,128)}, u32[]{:S(2)}) copy-start(f32[1,1,256,256]{3,2,1,0:T(8,128)} %meas_hbm.1) | copy-start | bytes 786436
  1.6 0.7 %copy-start.1 = (s32[1,16,2]{1,2,0:T(2,128)S(1)}, s32[1,16,2]{1,2,0:T(2,128)}, u32[]{:S(2)}) copy-start(s32[1,16,2]{1,2,0:T(2,128)} %param.4) | copy-start | bytes 388
  2.3 0.7 %copy-start.2 = (bf16[1,16,4]{1,2,0:T(4,128)(2,1)S(1)}, bf16[1,16,4]{1,2,0:T(4,128)(2,1)}, u32[]{:S(2)}) copy-start(bf16[1,16,4]{1,2,0:T(4,128)(2,1)} %param.5) | copy-start | bytes 388

commit v8 on v7

--- a/solution.py
+++ b/solution.py
@@ -30,12 +30,13 @@
 Z_BASE = 9
 Y_BASE = Z_BASE + 2 * VIEWS
 D_BASE = Y_BASE + 10 * VIEWS
-N_SEMS = D_BASE + 4
+N_SEMS = D_BASE + 4 * VIEWS
 
 PARTS = {
     "first": (HX, HX), "last": (TX, HX), "middle": (2 * HX, TX - 2 * HX),
     "top": (0, HX), "bottom": (HX + TX, HX),
 }
+DIRECT = {(2, "top"), (2, "bottom"), (3, "top"), (1, "bottom")}
 PART_ID = {"first": 0, "last": 1, "middle": 2, "top": 3, "bottom": 4}
 
 
@@ -153,10 +154,10 @@
                         self.region(slot, PARTS[rim], (HY, TY)),
                         self.region(slot, PARTS[halo], (HY, TY)), to_row(step),
                     )
-                    if slot == 2:
+                    if (slot, halo) in DIRECT:
                         for side, (src, dst, turn) in enumerate(((HY, HY + TY, -1), (TY, 0, 1))):
                             self.send(
-                                ("d", halo, side), D_BASE + 2 * k + side,
+                                ("d", slot, halo, side), D_BASE + 4 * slot + 2 * k + side,
                                 self.region(slot, PARTS[rim], (src, HY)),
                                 self.region(slot, PARTS[halo], (dst, HY)), to_corner(step, turn),
                             )
@@ -173,27 +174,29 @@
             self.spread(slot, part)
 
         def corners(self, slot):
-            for part, edge in (("top", 0), ("bottom", grid_x - 1)):
-                self.copies["z", slot, part].wait_recv()
-
-                @pl.when(gx == edge)
-                def _():
-                    start, size = PARTS[part]
-                    self.bufs[slot][pl.ds(start, size), pl.ds(HY, TY)] = jnp.zeros((size, TY), jnp.bfloat16)
-
-                self.columns(slot, part)
+            for halo, edge in (("top", 0), ("bottom", grid_x - 1)):
+                if (slot, halo) not in DIRECT:
+                    self.copies["z", slot, halo].wait_recv()
+                    start, size = PARTS[halo]
+
+                    @pl.when(gx == edge)
+                    def _():
+                        self.bufs[slot][pl.ds(start, size), pl.ds(HY, TY)] = jnp.zeros((size, TY), jnp.bfloat16)
+
+                    self.columns(slot, halo)
 
         def complete(self, slot):
-            if slot == 2:
-                for halo in ("top", "bottom"):
+            for halo, edge in (("top", 0), ("bottom", grid_x - 1)):
+                if (slot, halo) in DIRECT:
                     self.copies["z", slot, halo].wait_recv()
                     for side in (0, 1):
-                        self.copies["d", halo, side].wait_recv()
-                for halo, edge in (("top", 0), ("bottom", grid_x - 1)):
+                        self.copies["d", slot, halo, side].wait_recv()
+                    start, size = PARTS[halo]
+
                     @pl.when(gx == edge)
                     def _():
-                        start, size = PARTS[halo]
                         self.bufs[slot][pl.ds(start, size), :] = jnp.zeros((size, RY), jnp.bfloat16)
+
             for part in PARTS:
                 for side in (0, 1):
                     if ("y", slot, part, side) in self.copies:
@@ -475,13 +478,13 @@
     first.arrive(1, "middle")
     first.complete(0)
     stencil(e_refs[0], q_ref)
+    first.corners(3)
+    first.corners(1)
     first.arrive(2, "first")
     first.arrive(2, "last")
-    first.arrive(2, "middle")
-    first.corners(3)
-    first.corners(1)
     build(1)
     build_rows(1)
+    first.arrive(2, "middle")
     build(2)
     build_rows(2)
     for slot in (3, 1, 2):
@@ -499,10 +502,10 @@
         second.arrive(1, {"first": "last", "last": "first", "middle": "middle"}[part])
     second.complete(0)
     stencil(f_refs[0], p_ref)
+    second.corners(3)
+    second.corners(1)
     second.arrive(2, "first")
     second.arrive(2, "last")
-    second.corners(3)
-    second.corners(1)
     second.arrive(2, "middle")
     back(1, (0,))
     for slot in (3, 1, 2):
@@ -607,7 +610,7 @@
         compiler_params=pltpu.CompilerParams(
             collective_id=0, has_side_effects=True, vmem_limit_bytes=50 * 1024 * 1024
         ),
-    )(measured, jnp.transpose(shears, (0, 2, 1)), jnp.transpose(taps, (0, 2, 1)))
+    )(*[pltpu.with_memory_space_constraint(x, pltpu.HBM) for x in (measured, jnp.transpose(shears, (0, 2, 1)), jnp.transpose(taps, (0, 2, 1)))])
     return pl.pallas_call(
         write_kernel,
         name="write",

time: 67.8 us -> 64.3 us (0.948)
  local copies, waits for them, and re-layouts: 2.3 us -> 0 us
  Pallas kernels: 64.5 us -> 63.4 us
    unnamed x6 -> x0, local copies, waits for them, and re-layouts: 2.3 us -> none
    pallas_call x1, Pallas kernels: 62.3 us -> 61.2 us  [local(): pl.pallas_call(functools.partial(solve_kernel, grid_x), name='solve', out...]
where the time goes in v8:
time: 64.3 us; the launch traced here: 64.2 us
  Pallas kernels  63.4 us (99%)
  between operations  0.8 us (1%)
    pallas_call x1, Pallas kernels, local(): pl.pallas_call(functools.partial(solve_kernel, grid_x), name='solve', out...  61.2 us
    pallas_call x1, Pallas kernels, local(): pl.pallas_call(write_kernel, name='write', out_shape=(jax.ShapeDtypeStruc...  2.23 us

profile of v8, /device:TPU:1, one launch (start us, length us, event | category | flops | bytes accessed | tf_op | source)
XLA Modules:
  0.0 64.2 jit_solution(8926327226773226064)
XLA Ops:
  0.6 61.2 %solve.1 = (bf16[1,16,256,256]{3,2,1,0:T(8,128)(2,1)S(1)}, f32[1,1,256,256]{3,2,1,0:T(8,128)S(1)}) custom-call(f32[1,1,256,256]{3,2,1,0:T(8,128)} %meas_hbm.1, s32[1,2,16]{2,1,0:T(2,128)} %bitcast.2, bf16[1,4,16]{2,1,0:T(4,128)(2,1)} %bitcast.3), custom_call_target="tpu_custom_call" | custom-call | tf_op jit(solution)/shard_map/solve/pallas_call | solution.py:571
  61.8 2.2 %write.1 = (f32[1,16,256,256]{3,2,1,0:T(8,128)}, f32[1,1,256,256]{3,2,1,0:T(8,128)}) custom-call(bf16[1,16,256,256]{3,2,1,0:T(8,128)(2,1)S(1)} %get-tuple-element.4.vol_ref, f32[1,1,256,256]{3,2,1,0:T(8,128)S(1)} %get-tuple-element.5.res_ref), custom_call_target="tpu_custom_call" | custom-call | tf_op jit(solution)/shard_map/write/pallas_call | solution.py:614

commit v9 on v8

--- a/solution.py
+++ b/solution.py
@@ -356,7 +356,7 @@
 
         lax.fori_loop(0, TX // 64, rows, 0)
 
-    def apply(src_ref, out_ref, slot):
+    def columns_of(src_ref, slot):
         for z in range(PLANES):
             first_row = HX - 1 + sh_s[slot, 0, z] - sh_s[0, 0, z]
             start = lax.shift_right_logical(first_row, 4) * 16
@@ -364,17 +364,26 @@
                 src_ref[pl.ds(start, WINDOW), :], y_ref[(slot - 1) * PLANES + z], preferred_element_type=jnp.float32
             ).astype(jnp.bfloat16)
             strip = pl.ds(STRIP * (z % GROUP), STRIP)
-            strip_refs[0][z // GROUP, strip, :] = t[0:STRIP]
-            strip_refs[1][z // GROUP, strip, :] = t[128 : 128 + STRIP]
-        for half, t_ref in enumerate(strip_refs[0:2]):
+            strip_refs[2 * slot - 2][z // GROUP, strip, :] = t[0:STRIP]
+            strip_refs[2 * slot - 1][z // GROUP, strip, :] = t[128 : 128 + STRIP]
+
+    def rows_of(out_ref, slots):
+        for half in (0, 1):
             total = out_ref[pl.ds(128 * half, 128), :]
-            for g in range(PLANES // GROUP):
-                total = total + jnp.dot(
-                    x_ref[slot - 1, half, g],
-                    t_ref[g],
-                    preferred_element_type=jnp.float32,
-                )
+            for slot in slots:
+                for g in range(PLANES // GROUP):
+                    total = total + jnp.dot(
+                        x_ref[slot - 1, half, g],
+                        strip_refs[2 * slot - 2 + half][g],
+                        preferred_element_type=jnp.float32,
+                    )
             out_ref[pl.ds(128 * half, 128), :] = total
+
+    def others(exchange, out_ref):
+        for slot in (3, 1, 2):
+            exchange.complete(slot)
+            columns_of(exchange.bufs[slot], slot)
+        rows_of(out_ref, (3, 1, 2))
 
     def lanes(x):
         s = jnp.sum(x, axis=0, keepdims=True)
@@ -464,12 +473,12 @@
                 )
 
     fields()
+    first.arrive(3, "first")
+    first.arrive(1, "last")
+    first.corners(0)
     for copy in parameter_copies:
         copy.wait_recv()
     tables(0, VIEWS)
-    first.corners(0)
-    first.arrive(3, "first")
-    first.arrive(1, "last")
     build(3)
     build_rows(3)
     first.arrive(3, "last")
@@ -487,14 +496,14 @@
     first.arrive(2, "middle")
     build(2)
     build_rows(2)
-    for slot in (3, 1, 2):
-        first.complete(slot)
-        apply(e_refs[slot], q_ref, slot)
+    others(first, q_ref)
 
     second = Exchange(f_refs, 1)
     f_refs[0][pl.ds(HX, TX), pl.ds(HY, TY)] = q_ref[...].astype(jnp.bfloat16)
     second.along_views()
     second.own()
+    r0, q0 = e_refs[0][pl.ds(HX, TX), pl.ds(HY, TY)].astype(jnp.float32), q_ref[...]
+    known = [lanes(r0 * q0), lanes(q0 * q0)]
     back(0, (0,))
     second.corners(0)
     for part in ("first", "last", "middle"):
@@ -508,13 +517,11 @@
     second.arrive(2, "last")
     second.arrive(2, "middle")
     back(1, (0,))
-    for slot in (3, 1, 2):
-        second.complete(slot)
-        apply(f_refs[slot], p_ref, slot)
+    others(second, p_ref)
 
     r0 = e_refs[0][pl.ds(HX, TX), pl.ds(HY, TY)].astype(jnp.float32)
     q0, p = q_ref[...], p_ref[...]
-    sums = Sum([lanes(r0 * q0), lanes(q0 * q0), lanes(r0 * p), lanes(q0 * p), lanes(p * p)])
+    sums = Sum(known + [lanes(r0 * p), lanes(q0 * p), lanes(p * p)])
     sums.send(0)
     back(2, (0, 1))
     sums.receive(0)
@@ -591,7 +598,7 @@
             [pltpu.VMEM((PLANES, TX, TY), f32)] * 2,
             pltpu.VMEM((GROUP * VIEWS, RY, TY), bf16),
             pltpu.VMEM((GROUP, 128, VIEWS * STRIP), bf16),
-            [pltpu.VMEM((GROUP, VIEWS * STRIP, TY), bf16)] * 4,
+            [pltpu.VMEM((GROUP, VIEWS * STRIP, TY), bf16)] * 6,
             pltpu.VMEM((VIEWS, 8, 128), jnp.int32),
             pltpu.VMEM((VIEWS, 8, 128), f32),
             pltpu.SMEM((VIEWS, 8, 128), jnp.int32),

time: 64.3 us -> 64.7 us (level)
  no operation moved by 1% of the time
where the time goes in v9:
time: 64.7 us; the launch traced here: 64.6 us
  Pallas kernels  63.8 us (99%)
  between operations  0.8 us (1%)
    pallas_call x1, Pallas kernels, local(): pl.pallas_call(functools.partial(solve_kernel, grid_x), name='solve', out...  61.6 us
    pallas_call x1, Pallas kernels, local(): pl.pallas_call(write_kernel, name='write', out_shape=(jax.ShapeDtypeStruc...  2.23 us

profile of v9, /device:TPU:1, one launch (start us, length us, event | category | flops | bytes accessed | tf_op | source)
XLA Modules:
  0.0 64.6 jit_solution(13565971129646056466)
XLA Ops:
  0.6 61.6 %solve.1 = (bf16[1,16,256,256]{3,2,1,0:T(8,128)(2,1)S(1)}, f32[1,1,256,256]{3,2,1,0:T(8,128)S(1)}) custom-call(f32[1,1,256,256]{3,2,1,0:T(8,128)} %meas_hbm.1, s32[1,2,16]{2,1,0:T(2,128)} %bitcast.2, bf16[1,4,16]{2,1,0:T(4,128)(2,1)} %bitcast.3), custom_call_target="tpu_custom_call" | custom-call | tf_op jit(solution)/shard_map/solve/pallas_call | solution.py:578
  62.2 2.2 %write.1 = (f32[1,16,256,256]{3,2,1,0:T(8,128)}, f32[1,1,256,256]{3,2,1,0:T(8,128)}) custom-call(bf16[1,16,256,256]{3,2,1,0:T(8,128)(2,1)S(1)} %get-tuple-element.4.vol_ref, f32[1,1,256,256]{3,2,1,0:T(8,128)S(1)} %get-tuple-element.5.res_ref), custom_call_target="tpu_custom_call" | custom-call | tf_op jit(solution)/shard_map/write/pallas_call | solution.py:621

commit v10 on v8

--- a/solution.py
+++ b/solution.py
@@ -49,7 +49,7 @@
     meas_hbm, sh_hbm, tp_hbm,
     vol_ref, res_ref,
     meas_ref, sh_ref, tp_ref, e_refs, f_refs, field_ref, y_ref, x_ref, q_ref, p_ref, back_refs, by_ref, bx_ref, strip_refs,
-    sh_v, tp_v, sh_s, tp_s, ra_ref, rb_ref, rc_ref,
+    sh_v, tp_v, sh_s, tp_s, ra_ref, rb_ref,
     send_sems, recv_sems, p_send, p_recv, p_local, a_send, a_recv,
 ):
     tile = lax.axis_index("tile")
@@ -72,11 +72,29 @@
     def to_corner(row_step, col_step):
         return at(ring(gx, row_step, grid_x), ring(gy, col_step, GRID_Y), view)
 
+    chips = GRID_Y // 2
+    core = lax.rem(gy, 2)
+
+    def to_view_chip(step):
+        return at(gx, ring(gy, 2 * step[1], GRID_Y), ring(view, step[0], VIEWS))
+
+    def to_row_core(step):
+        return at(ring(gx, step[0], grid_x), gy + step[1] * (1 - 2 * core), view)
+
+    def hops(step, sizes):
+        return sum(min(k, n - k) for k, n in zip(step, sizes))
+
+    def group(sizes):
+        steps = [(a, b) for a in range(sizes[0]) for b in range(sizes[1]) if a + b]
+        return sorted(steps, key=lambda step: -hops(step, sizes))
+
+    view_chips, row_cores = group((VIEWS, chips)), group((grid_x, 2))
+
+    next_chip = ring(gy, 2 * core - 1, GRID_Y)
     partners = (
-        [to_view(s) for s in range(1, VIEWS)]
-        + [to_row(s) for s in range(1, grid_x)]
-        + [to_col(s) for s in range(1, GRID_Y)]
-        + [to_corner(r, c) for r in (-1, 1) for c in (-1, 1)]
+        [to_view_chip(step) for step in view_chips]
+        + [to_row_core(step) for step in row_cores]
+        + [at(ring(gx, r, grid_x), next_chip, view) for r in (-1, 0, 1)]
     )
     barrier = pltpu.get_barrier_semaphore()
     for partner in partners:
@@ -383,22 +401,21 @@
     class Sum:
         def __init__(self, rows):
             self.stages = (
-                (ra_ref, view, VIEWS, to_view, 0),
-                (rb_ref, gy, GRID_Y, to_col, VIEWS),
-                (rc_ref, gx, grid_x, to_row, VIEWS + GRID_Y),
+                (ra_ref, view * chips + gy // 2, VIEWS * chips, view_chips, to_view_chip, 0),
+                (rb_ref, gx * 2 + core, grid_x * 2, row_cores, to_row_core, VIEWS * chips),
             )
             self.copies = []
             pad = jnp.zeros((8 - len(rows), 128), jnp.float32)
             self.value = jnp.concatenate(list(rows) + [pad], axis=0)
 
         def send(self, stage):
-            ref, me, size, to, base = self.stages[stage]
+            ref, me, size, steps, to, base = self.stages[stage]
             ref[me] = self.value
             self.current = []
-            for step in sorted(range(1, size), key=lambda k: -min(k, size - k)):
+            for k, step in enumerate(steps):
                 copy = pltpu.make_async_remote_copy(
                     src_ref=ref.at[me], dst_ref=ref.at[me],
-                    send_sem=a_send.at[base + step], recv_sem=a_recv.at[base + step],
+                    send_sem=a_send.at[base + k], recv_sem=a_recv.at[base + k],
                     device_id=to(step), device_id_type=MESH,
                 )
                 copy.start()
@@ -406,7 +423,7 @@
             self.copies += self.current
 
         def receive(self, stage):
-            ref, me, size, to, base = self.stages[stage]
+            ref, me, size, steps, to, base = self.stages[stage]
             for copy in self.current:
                 copy.wait_recv()
             total = ref[0]
@@ -520,11 +537,9 @@
     sums.receive(0)
     sums.send(1)
     back(3, (0, 1))
-    sums.receive(1)
-    sums.send(2)
     back(0, (1,))
     back(1, (1,))
-    sums.receive(2)
+    sums.receive(1)
     r0q0, q0q0, r0p, q0p, pp = [sums.row(i) for i in range(5)]
     gamma0 = r0q0
     alpha0 = gamma0 / (q0q0 + TINY)
@@ -566,7 +581,7 @@
 def local(grid_x, measured, shears, taps):
     f32, bf16 = jnp.float32, jnp.bfloat16
     vmem = pl.BlockSpec(memory_space=pltpu.VMEM)
-    partners = VIEWS + GRID_Y + grid_x
+    partners = VIEWS * GRID_Y // 2 + 2 * grid_x
     hbm = pl.BlockSpec(memory_space=pltpu.HBM)
     volume, residual = pl.pallas_call(
         functools.partial(solve_kernel, grid_x),
@@ -596,9 +611,8 @@
             pltpu.VMEM((VIEWS, 8, 128), f32),
             pltpu.SMEM((VIEWS, 8, 128), jnp.int32),
             pltpu.SMEM((VIEWS, 8, 128), f32),
-            pltpu.VMEM((VIEWS, 8, 128), f32),
-            pltpu.VMEM((GRID_Y, 8, 128), f32),
-            pltpu.VMEM((grid_x, 8, 128), f32),
+            pltpu.VMEM((VIEWS * GRID_Y // 2, 8, 128), f32),
+            pltpu.VMEM((grid_x * 2, 8, 128), f32),
             pltpu.SemaphoreType.DMA((2, N_SEMS)),
             pltpu.SemaphoreType.DMA((2, N_SEMS)),
             pltpu.SemaphoreType.DMA((2, VIEWS)),

time: 64.3 us -> 65.5 us (1.019)
  Pallas kernels: 63.4 us -> 64.6 us
    pallas_call x1, Pallas kernels: 61.2 us -> 62.4 us  [local(): pl.pallas_call(functools.partial(solve_kernel, grid_x), name='solve', out...]
where the time goes in v10:
time: 65.5 us; the launch traced here: 65.4 us
  Pallas kernels  64.6 us (99%)
  between operations  0.8 us (1%)
    pallas_call x1, Pallas kernels, local(): pl.pallas_call(functools.partial(solve_kernel, grid_x), name='solve', out...  62.4 us
    pallas_call x1, Pallas kernels, local(): pl.pallas_call(write_kernel, name='write', out_shape=(jax.ShapeDtypeStruc...  2.23 us

profile of v10, /device:TPU:1, one launch (start us, length us, event | category | flops | bytes accessed | tf_op | source)
XLA Modules:
  0.0 65.4 jit_solution(4277234595575248726)
XLA Ops:
  0.6 62.4 %solve.1 = (bf16[1,16,256,256]{3,2,1,0:T(8,128)(2,1)S(1)}, f32[1,1,256,256]{3,2,1,0:T(8,128)S(1)}) custom-call(f32[1,1,256,256]{3,2,1,0:T(8,128)} %meas_hbm.1, s32[1,2,16]{2,1,0:T(2,128)} %bitcast.2, bf16[1,4,16]{2,1,0:T(4,128)(2,1)} %bitcast.3), custom_call_target="tpu_custom_call" | custom-call | tf_op jit(solution)/shard_map/solve/pallas_call | solution.py:586
  63.0 2.2 %write.1 = (f32[1,16,256,256]{3,2,1,0:T(8,128)}, f32[1,1,256,256]{3,2,1,0:T(8,128)}) custom-call(bf16[1,16,256,256]{3,2,1,0:T(8,128)(2,1)S(1)} %get-tuple-element.4.vol_ref, f32[1,1,256,256]{3,2,1,0:T(8,128)S(1)} %get-tuple-element.5.res_ref), custom_call_target="tpu_custom_call" | custom-call | tf_op jit(solution)/shard_map/write/pallas_call | solution.py:628
